TPU v7x, 32 devices: a whole 2x2x4 slice. The times are simulated.
32 devices in a mesh: dp: 4 (over y, x), expert: 8 (over z, core).
Axes of the slice: x: 2, y: 2, z: 4, core: 2. Of those that a mesh axis runs over, the one named last changes fastest.
Arguments:
- block_input: bfloat16 [4096, 512], P(('dp', 'expert')), may hold values from -6 to 6
- cotangent: bfloat16 [4096, 512], P(('dp', 'expert')), may hold values from -6 to 6
- lengths: int32 [4, 6], P('dp'), may hold values from 1 to 512, 896 in all within a row
- run_loops: int32 [4096], P('dp'), may hold values from 1 to 3
- attn_routes: int32 [3, 4096, 4], P(None, 'dp'), may hold values from 0 to 7, all different within a row; in each aligned block of 1024 rows (0 to 1023, 1024 to 2047, ..., all dimensions but the last counted through in order) at most 640 rows name the same one
- ffn_routes: int32 [3, 4096, 2], P(None, 'dp'), may hold values from 0 to 7, all different within a row; in each aligned block of 1024 rows (0 to 1023, 1024 to 2047, ..., all dimensions but the last counted through in order) at most 320 rows name the same one
- shared_vectors: float32 [5, 512], replicated, as said below
- shared_moment: float32 [5, 512], replicated
- shared_second: float32 [5, 512], replicated, as said below
- key_value: float32 [512, 128], replicated, may hold values from -0.25 to 0.25
- kv_moment: float32 [512, 128], replicated, may hold values from -112 to 112
- kv_second: float32 [512, 128], replicated, may hold values from 358.4 to 1433.6
- router_weights: float32 [512, 16], replicated, may hold values from -0.15625 to 0.15625
- router_moment: float32 [512, 16], replicated, may hold values from -16 to 16
- router_second: float32 [512, 16], replicated, may hold values from 96.0512 to 387.072
- attn_weights: float32 [8, 512, 128], P('expert', 'dp')
- attn_moment: float32 [8, 512, 128], P('expert', 'dp')
- attn_second: float32 [8, 512, 128], P('expert', 'dp'), as said below
- up_weights: float32 [8, 512, 2048], P('expert', 'dp'), may hold values from -0.25 to 0.25
- up_moment: float32 [8, 512, 2048], P('expert', 'dp'), may hold values from -4 to 4
- up_second: float32 [8, 512, 2048], P('expert', 'dp'), may hold values from 0.25088 to 1.00352
- down_weights: float32 [8, 512, 2048], P('expert', 'dp'), may hold values from -0.125 to 0.125
- down_moment: float32 [8, 512, 2048], P('expert', 'dp'), may hold values from -8 to 8
- down_second: float32 [8, 512, 2048], P('expert', 'dp'), may hold values from 1.792 to 7.168
Outputs:
- output: float32 [4096, 512], P(('dp', 'expert'))
- input_grad: float32 [4096, 512], P(('dp', 'expert'))
- shared_new: float32 [5, 512], replicated
- shared_moment_new: float32 [5, 512], replicated
- shared_second_new: float32 [5, 512], replicated
- kv_new: float32 [512, 128], replicated
- kv_moment_new: float32 [512, 128], replicated
- kv_second_new: float32 [512, 128], replicated
- router_new: float32 [512, 16], replicated
- router_moment_new: float32 [512, 16], replicated
- router_second_new: float32 [512, 16], replicated
- attn_new: float32 [8, 512, 128], P('expert', 'dp')
- attn_moment_new: float32 [8, 512, 128], P('expert', 'dp')
- attn_second_new: float32 [8, 512, 128], P('expert', 'dp')
- attn_copy: bfloat16 [8, 512, 128], P('expert', 'dp')
- up_new: float32 [8, 512, 2048], P('expert', 'dp')
- up_moment_new: float32 [8, 512, 2048], P('expert', 'dp')
- up_second_new: float32 [8, 512, 2048], P('expert', 'dp')
- up_copy: bfloat16 [8, 512, 2048], P('expert', 'dp')
- down_new: float32 [8, 512, 2048], P('expert', 'dp')
- down_moment_new: float32 [8, 512, 2048], P('expert', 'dp')
- down_second_new: float32 [8, 512, 2048], P('expert', 'dp')
- down_copy: bfloat16 [8, 512, 2048], P('expert', 'dp')
Inputs may be any that keep to these rules, and one draw needn't show every extreme that they name: The lengths of one data device sum to 896; the remaining slots are padding. `attn_routes`: each row names 4 different experts; in each loop at most 640 rows of one data device name one expert, and that many do in some blocks. `ffn_routes`: each row names 2 different experts; in each loop at most 320 rows of one data device name one expert, and that many do in some blocks. `shared_vectors`: gains positive, biases and the halting weight of both signs. `shared_second`: Positive. `attn_second`: Positive.
All inputs are finite; a program needn't handle non-finite values.
Results may differ from a plain program's by a relative error of at most 0.025.
The roundings to bfloat16 on the way count: a program that leaves them out, or rounds other values in their place, can miss the bound.
Values may be sent and summed in bfloat16 or wider, within the bound.
A program may use at most 192 MiB of HBM per device.

v0:
```python
import math

import jax
import jax.numpy as jnp
from jax import lax
from jax.sharding import PartitionSpec as P

D = 512
HD = 64
FF = 2048
ATT_DEV = 1
FFN_DEV = 1
KATT = 4
KFF = 2
LOOPS = 3
STEP = 10


ln_eps = 1e-05
beta_one = 0.9
beta_two = 0.999
adam_eps = 1e-08
decay_rate = 0.01
masked_score = -1e30


def layer_norm(values, gain_row, offset):
    centre = values - jnp.mean(values, axis=-1, keepdims=True)
    spread = jnp.mean(centre * centre, axis=-1, keepdims=True)
    return centre * lax.rsqrt(spread + ln_eps) * gain_row + offset


def compact(selected, capacity):
    total_rows = selected.shape[0]
    as_ints = selected.astype(jnp.int32)
    target = jnp.where(selected, jnp.cumsum(as_ints) - 1, capacity)
    places = (
        jnp.zeros((capacity + 1,), jnp.int32)
        .at[target]
        .set(jnp.arange(total_rows, dtype=jnp.int32))
    )
    filled = (jnp.arange(capacity, dtype=jnp.int32) < jnp.sum(as_ints)).astype(jnp.float32)
    return (places[:capacity], filled)


def dense_gates(logits, chosen, width):
    picked = jnp.take_along_axis(logits, chosen, axis=1)
    weights = jax.nn.softmax(picked, axis=-1)
    onehot = (chosen[:, :, None] == jnp.arange(width, dtype=jnp.int32)[None, None, :]).astype(
        jnp.float32
    )
    return jnp.sum(weights[:, :, None] * onehot, axis=1)


def halt_mix(states, halt_weight):
    remain = jnp.ones((states[0].shape[0], 1), jnp.float32)
    result = jnp.zeros_like(states[0])
    last = len(states) - 1
    for number, current in enumerate(states):
        if number < last:
            chance = jax.nn.sigmoid(jnp.sum(current * halt_weight, axis=-1, keepdims=True))
            result = result + remain * chance * current
            remain = remain * (1.0 - chance)
        else:
            result = result + remain * current
    return result


def contract(left, right, left_dim, right_dim):
    return lax.dot_general(
        left, right, (((left_dim,), (right_dim,)), ((), ())), preferred_element_type=jnp.float32
    )


def adam_update(weight, moment, second, grad, rate, decay):
    moment_new = beta_one * moment + (1.0 - beta_one) * grad
    second_new = beta_two * second + (1.0 - beta_two) * grad * grad
    moment_hat = moment_new / (1.0 - beta_one**STEP)
    second_hat = second_new / (1.0 - beta_two**STEP)
    weight_new = weight - rate * (moment_hat / (jnp.sqrt(second_hat) + adam_eps) + decay * weight)
    return (weight_new, moment_new, second_new)


def per_device(
    block_input,
    cotangent,
    lengths,
    run_loops,
    attn_routes,
    ffn_routes,
    shared_vectors,
    shared_moment,
    shared_second,
    key_value,
    kv_moment,
    kv_second,
    router_weights,
    router_moment,
    router_second,
    attn_weights,
    attn_moment,
    attn_second,
    up_weights,
    up_moment,
    up_second,
    down_weights,
    down_moment,
    down_second,
):
    expert_count = lax.axis_size("expert")
    expert_id = lax.axis_index("expert")
    att_count = ATT_DEV * expert_count
    ffn_count = FFN_DEV * expert_count
    own_rows = block_input.shape[0]
    width = block_input.shape[1]
    row_total = run_loops.shape[0]
    head_width = attn_weights.shape[2] // 2
    scale = head_width ** (-0.5)
    att_cap = min(row_total, 5 * row_total * KATT // (4 * att_count))
    ffn_cap = 5 * row_total * KFF // (4 * ffn_count)
    block_rows = att_cap // max(1, att_cap // 512)
    block_count = att_cap // block_rows
    first_row = expert_id * own_rows
    positions = jnp.arange(row_total, dtype=jnp.int32)
    bounds = jnp.cumsum(lengths[0])
    segment = jnp.sum((positions[:, None] >= bounds[None, :]).astype(jnp.int32), axis=1)
    valid = segment < lengths.shape[1]
    gathered = (
        lax.all_gather(attn_weights.astype(jnp.bfloat16), "dp", axis=1, tiled=True),
        lax.all_gather(up_weights.astype(jnp.bfloat16), "dp", axis=1, tiled=True),
        lax.all_gather(down_weights.astype(jnp.bfloat16), "dp", axis=1, tiled=True),
    )
    attn_local = gathered[0][0]
    up_local = gathered[1][0]
    down_local = gathered[2][0]
    query_weight = attn_local[:, :head_width]
    out_weight = attn_local[:, head_width:]
    kv_low = key_value.astype(jnp.bfloat16)
    router_low = router_weights.astype(jnp.bfloat16)
    att_router = router_low[:, :att_count]
    ffn_router = router_low[:, att_count:]

    def block_scores(query_blk, place_blk, key_rows):
        raw = contract(query_blk, key_rows, 1, 1) * scale
        allowed = (segment[place_blk][:, None] == segment[None, :]) & (
            positions[None, :] <= place_blk[:, None]
        )
        return jnp.where(allowed, raw, masked_score)

    def attn_prep(normed_all, chosen, running):
        kv_vals = jnp.dot(normed_all, kv_low, preferred_element_type=jnp.float32).astype(
            jnp.bfloat16
        )
        logits = jnp.dot(normed_all, att_router, preferred_element_type=jnp.float32)
        mine = dense_gates(logits, chosen, att_count)[:, expert_id]
        selected = jnp.any(chosen == expert_id, axis=1) & running
        places, filled = compact(selected, att_cap)
        query_rows = normed_all[places]
        query = jnp.dot(query_rows, query_weight, preferred_element_type=jnp.float32).astype(
            jnp.bfloat16
        )
        return (kv_vals, places, mine[places] * filled, filled, query_rows, query)

    def attention_backward(normed_all, grad_all, totals, chosen, running):
        kv_vals, places, weights, filled, query_rows, query = attn_prep(normed_all, chosen, running)
        key_rows = kv_vals[:, :head_width]
        value_rows = kv_vals[:, head_width:]
        grad_rows = grad_all[places]
        scaled = (grad_rows * weights[:, None]).astype(jnp.bfloat16)

        def backward_block(carry, items):
            key_grad, value_grad, out_w_grad = carry
            query_blk, place_blk, total_blk, scaled_blk, grad_blk = items
            prob = jnp.exp(block_scores(query_blk, place_blk, key_rows) - total_blk[:, None])
            prob_low = prob.astype(jnp.bfloat16)
            out_blk = jnp.dot(prob_low, value_rows, preferred_element_type=jnp.float32).astype(
                jnp.bfloat16
            )
            part = contract(out_blk, out_weight, 1, 1)
            gate_grad = jnp.sum(grad_blk * part, axis=1)
            out_w_grad = out_w_grad + contract(scaled_blk, out_blk, 0, 0)
            out_grad = jnp.dot(scaled_blk, out_weight, preferred_element_type=jnp.float32).astype(
                jnp.bfloat16
            )
            prob_grad = contract(out_grad, value_rows, 1, 1)
            centre = jnp.sum(prob * prob_grad, axis=1, keepdims=True)
            score_grad = (prob * (prob_grad - centre)).astype(jnp.bfloat16)
            query_grad = (
                jnp.dot(score_grad, key_rows, preferred_element_type=jnp.float32) * scale
            ).astype(jnp.bfloat16)
            key_grad = key_grad + contract(score_grad, query_blk, 0, 0)
            value_grad = value_grad + contract(prob_low, out_grad, 0, 0)
            return ((key_grad, value_grad, out_w_grad), (query_grad, gate_grad))

        start = (
            jnp.zeros((row_total, head_width), jnp.float32),
            jnp.zeros((row_total, head_width), jnp.float32),
            jnp.zeros((width, head_width), jnp.float32),
        )
        items = (
            query.reshape(block_count, block_rows, head_width),
            places.reshape(block_count, block_rows),
            totals.reshape(block_count, block_rows),
            scaled.reshape(block_count, block_rows, width),
            grad_rows.reshape(block_count, block_rows, width),
        )
        (key_grad, value_grad, out_w_grad), (query_grads, gate_grads) = lax.scan(
            backward_block, start, items
        )
        query_grads = query_grads.reshape(att_cap, head_width)
        gate_grads = gate_grads.reshape(att_cap) * filled
        query_w_grad = contract(query_rows, query_grads, 0, 0)
        row_grads = contract(query_grads, query_weight, 1, 1)
        input_part = jnp.zeros((row_total, width), jnp.float32).at[places].add(row_grads)
        gate_col = jnp.zeros((row_total,), jnp.float32).at[places].add(gate_grads)
        gate_mat = (
            gate_col[:, None]
            * (jnp.arange(att_count, dtype=jnp.int32) == expert_id).astype(jnp.float32)[None, :]
        )
        kv_part = jnp.concatenate([key_grad * scale, value_grad], axis=1)
        return (
            (input_part, kv_part, gate_mat),
            jnp.concatenate([query_w_grad, out_w_grad], axis=1),
        )

    def ffn_prep(second_all, chosen, running):
        logits = jnp.dot(second_all, ffn_router, preferred_element_type=jnp.float32)
        mine = dense_gates(logits, chosen, ffn_count)[:, expert_id]
        selected = jnp.any(chosen == expert_id, axis=1) & running
        places, filled = compact(selected, ffn_cap)
        rows_in = second_all[places]
        inner = jnp.dot(rows_in, up_local, preferred_element_type=jnp.float32)
        hidden = jax.nn.gelu(inner).astype(jnp.bfloat16)
        return (places, mine[places] * filled, filled, rows_in, inner, hidden)

    def ffn_backward(second_all, grad_all, chosen, running):
        places, weights, filled, rows_in, inner, hidden = ffn_prep(second_all, chosen, running)
        part = contract(hidden, down_local, 1, 1)
        grad_rows = grad_all[places]
        gate_grads = jnp.sum(grad_rows * part, axis=1) * filled
        scaled = (grad_rows * weights[:, None]).astype(jnp.bfloat16)
        down_grad = contract(scaled, hidden, 0, 0)
        hidden_grad = jnp.dot(scaled, down_local, preferred_element_type=jnp.float32)
        gelu_out, gelu_back = jax.vjp(jax.nn.gelu, inner)
        inner_grad = gelu_back(hidden_grad)[0].astype(jnp.bfloat16)
        up_grad = contract(rows_in, inner_grad, 0, 0)
        row_grads = contract(inner_grad, up_local, 1, 1)
        input_part = jnp.zeros((row_total, width), jnp.float32).at[places].add(row_grads)
        gate_col = jnp.zeros((row_total,), jnp.float32).at[places].add(gate_grads)
        gate_mat = (
            gate_col[:, None]
            * (jnp.arange(ffn_count, dtype=jnp.int32) == expert_id).astype(jnp.float32)[None, :]
        )
        return ((input_part, gate_mat), up_grad, down_grad)

    def router_back(rows_low, chosen_own, gate_grad, count_cols, weight_cols):
        logits = jnp.dot(rows_low, weight_cols, preferred_element_type=jnp.float32)

        def gating(logit_vals):
            return dense_gates(logit_vals, chosen_own, count_cols)

        gate_vals, gate_back = jax.vjp(gating, logits)
        logit_grad = gate_back(gate_grad)[0].astype(jnp.bfloat16)
        return (contract(rows_low, logit_grad, 0, 0), contract(logit_grad, weight_cols, 1, 1))

    gain_one = shared_vectors[0]
    bias_one = shared_vectors[1]
    gain_two = shared_vectors[2]
    bias_two = shared_vectors[3]
    halt_weight = shared_vectors[4]
    state = block_input.astype(jnp.float32)
    inputs, mixes, totals_all, kept_one, kept_two, states = ([], [], [], [], [], [])
    for loop_id in range(LOOPS):
        running = valid & (loop_id < run_loops)
        running_own = lax.dynamic_slice_in_dim(running, first_row, own_rows).astype(jnp.float32)[
            :, None
        ]
        normed = layer_norm(state, gain_one, bias_one).astype(jnp.bfloat16)
        normed_all = lax.all_gather(normed, "expert", axis=0, tiled=True)
        (
            attention_kv_vals,
            attention_places,
            attention_weights,
            attention_filled,
            attention_query_rows,
            attention_query,
        ) = attn_prep(normed_all, attn_routes[loop_id], running)
        attention_key_rows = attention_kv_vals[:, :head_width]
        attention_value_rows = attention_kv_vals[:, head_width:]

        def forward_block(items):
            query_blk, place_blk = items
            scores = block_scores(query_blk, place_blk, attention_key_rows)
            top = jnp.max(scores, axis=1, keepdims=True)
            log_total = top[:, 0] + jnp.log(jnp.sum(jnp.exp(scores - top), axis=1))
            prob = jnp.exp(scores - log_total[:, None])
            out_blk = jnp.dot(
                prob.astype(jnp.bfloat16), attention_value_rows, preferred_element_type=jnp.float32
            )
            return (out_blk.astype(jnp.bfloat16), log_total)

        out_rows, attention_totals = lax.map(
            forward_block,
            (
                attention_query.reshape(block_count, block_rows, head_width),
                attention_places.reshape(block_count, block_rows),
            ),
        )
        out_rows = out_rows.reshape(att_cap, head_width)
        attention_part = contract(out_rows, out_weight, 1, 1)
        contrib = (
            jnp.zeros((row_total, width), jnp.float32)
            .at[attention_places]
            .add(attention_part * attention_weights[:, None])
        )
        contrib, log_totals = (contrib, attention_totals.reshape(att_cap))
        mixed = lax.psum_scatter(contrib, "expert", scatter_dimension=0, tiled=True)
        middle = state + mixed
        second = layer_norm(middle, gain_two, bias_two).astype(jnp.bfloat16)
        second_all = lax.all_gather(second, "expert", axis=0, tiled=True)
        ffn_places, ffn_weights, ffn_filled, ffn_rows_in, ffn_inner, ffn_hidden = ffn_prep(
            second_all, ffn_routes[loop_id], running
        )
        ffn_part = contract(ffn_hidden, down_local, 1, 1)
        ffn_contrib = (
            jnp.zeros((row_total, width), jnp.float32)
            .at[ffn_places]
            .add(ffn_part * ffn_weights[:, None])
        )
        ffn_out = lax.psum_scatter(ffn_contrib, "expert", scatter_dimension=0, tiled=True)
        inputs.append(state)
        mixes.append(mixed)
        totals_all.append(log_totals)
        kept_one.append(normed_all)
        kept_two.append(second_all)
        state = jnp.where(running_own > 0.0, middle + ffn_out, state)
        states.append(state)
    output, halt_back = jax.vjp(halt_mix, tuple(states), halt_weight)
    state_grads, halt_grad = halt_back(cotangent.astype(jnp.float32))
    attn_acc = jnp.zeros((width, 2 * head_width), jnp.float32)
    up_acc = jnp.zeros((width, up_local.shape[1]), jnp.float32)
    down_acc = jnp.zeros((width, down_local.shape[1]), jnp.float32)
    kv_acc = jnp.zeros((width, 2 * head_width), jnp.float32)
    router_att_acc = jnp.zeros((width, att_count), jnp.float32)
    router_ffn_acc = jnp.zeros((width, ffn_count), jnp.float32)
    gain_one_acc = jnp.zeros((width,), jnp.float32)
    bias_one_acc = jnp.zeros((width,), jnp.float32)
    gain_two_acc = jnp.zeros((width,), jnp.float32)
    bias_two_acc = jnp.zeros((width,), jnp.float32)
    carry_grad = jnp.zeros((own_rows, width), jnp.float32)
    for loop_id in reversed(range(LOOPS)):
        running = valid & (loop_id < run_loops)
        running_own = lax.dynamic_slice_in_dim(running, first_row, own_rows).astype(jnp.float32)[
            :, None
        ]
        chosen_att = attn_routes[loop_id]
        chosen_ffn = ffn_routes[loop_id]
        chosen_att_own = lax.dynamic_slice_in_dim(chosen_att, first_row, own_rows, axis=0)
        chosen_ffn_own = lax.dynamic_slice_in_dim(chosen_ffn, first_row, own_rows, axis=0)
        state_in = inputs[loop_id]
        middle = state_in + mixes[loop_id]
        after_grad = state_grads[loop_id] + carry_grad
        branch_grad = after_grad * running_own
        pass_grad = after_grad * (1.0 - running_own)
        normed = layer_norm(state_in, gain_one, bias_one).astype(jnp.bfloat16)
        second = layer_norm(middle, gain_two, bias_two).astype(jnp.bfloat16)
        normed_all = lax.all_gather(normed, "expert", axis=0, tiled=True)
        second_all = lax.all_gather(second, "expert", axis=0, tiled=True)
        grad_all = lax.all_gather(branch_grad, "expert", axis=0, tiled=True)
        (ffn_in_part, ffn_gate_mat), up_grad, down_grad = ffn_backward(
            second_all, grad_all, chosen_ffn, running
        )
        up_acc = up_acc + up_grad
        down_acc = down_acc + down_grad
        second_grad, ffn_gate_grad = (
            lax.psum_scatter(ffn_in_part, "expert", scatter_dimension=0, tiled=True),
            lax.psum_scatter(ffn_gate_mat, "expert", scatter_dimension=0, tiled=True),
        )
        router_grad, row_grad = router_back(
            second, chosen_ffn_own, ffn_gate_grad, ffn_count, ffn_router
        )
        router_ffn_acc = router_ffn_acc + router_grad
        second_grad = second_grad + row_grad
        norm_vals, norm_back = jax.vjp(layer_norm, middle, gain_two, bias_two)
        middle_part, gain_grad, bias_grad = norm_back(second_grad)
        gain_two_acc = gain_two_acc + gain_grad
        bias_two_acc = bias_two_acc + bias_grad
        middle_grad = middle_part + branch_grad
        attn_grad_all = lax.all_gather(middle_grad, "expert", axis=0, tiled=True)
        (attn_in_part, kv_part, att_gate_mat), attn_grad = attention_backward(
            normed_all, attn_grad_all, totals_all[loop_id], chosen_att, running
        )
        normed_grad, kv_grad, att_gate_grad = (
            lax.psum_scatter(attn_in_part, "expert", scatter_dimension=0, tiled=True),
            lax.psum_scatter(kv_part, "expert", scatter_dimension=0, tiled=True),
            lax.psum_scatter(att_gate_mat, "expert", scatter_dimension=0, tiled=True),
        )
        attn_acc = attn_acc + attn_grad
        kv_low_grad = kv_grad.astype(jnp.bfloat16)
        kv_acc = kv_acc + contract(normed, kv_low_grad, 0, 0)
        normed_grad = normed_grad + contract(kv_low_grad, kv_low, 1, 1)
        router_grad, row_grad = router_back(
            normed, chosen_att_own, att_gate_grad, att_count, att_router
        )
        router_att_acc = router_att_acc + router_grad
        normed_grad = normed_grad + row_grad
        norm_vals, first_back = jax.vjp(layer_norm, state_in, gain_one, bias_one)
        in_part, gain_grad, bias_grad = first_back(normed_grad)
        gain_one_acc = gain_one_acc + gain_grad
        bias_one_acc = bias_one_acc + bias_grad
        carry_grad = pass_grad + middle_grad + in_part
    attn_sum, up_sum, down_sum = (
        lax.psum_scatter(attn_acc, "dp", scatter_dimension=0, tiled=True),
        lax.psum_scatter(up_acc, "dp", scatter_dimension=0, tiled=True),
        lax.psum_scatter(down_acc, "dp", scatter_dimension=0, tiled=True),
    )
    shared_part = jnp.stack(
        [gain_one_acc, bias_one_acc, gain_two_acc, bias_two_acc, halt_grad], axis=0
    )
    router_part = jnp.concatenate([router_att_acc, router_ffn_acc], axis=1)
    shared_sum, kv_sum, router_sum = lax.psum((shared_part, kv_acc, router_part), ("dp", "expert"))
    shared_rates = jnp.array([6.0, 6.0, 6.0, 6.0, 20.0 / math.sqrt(D)], dtype=jnp.float32)[:, None]
    attn_rates = jnp.concatenate(
        [
            jnp.full((HD,), 25.0 / math.sqrt(D), jnp.float32),
            jnp.full((HD,), 50.0 / math.sqrt(HD), jnp.float32),
        ]
    )
    shared_new = adam_update(
        shared_vectors, shared_moment, shared_second, shared_sum, shared_rates, 0.0
    )
    kv_new = adam_update(key_value, kv_moment, kv_second, kv_sum, 20.0 / math.sqrt(D), decay_rate)
    router_new = adam_update(
        router_weights,
        router_moment,
        router_second,
        router_sum,
        50.0 / math.sqrt(3 * D),
        decay_rate,
    )
    attn_new = adam_update(
        attn_weights, attn_moment, attn_second, attn_sum[None], attn_rates, decay_rate
    )
    up_new = adam_update(
        up_weights, up_moment, up_second, up_sum[None], 14.0 / math.sqrt(D), decay_rate
    )
    down_new = adam_update(
        down_weights, down_moment, down_second, down_sum[None], 17.0 / math.sqrt(FF), decay_rate
    )
    return (
        output,
        carry_grad,
        shared_new[0],
        shared_new[1],
        shared_new[2],
        kv_new[0],
        kv_new[1],
        kv_new[2],
        router_new[0],
        router_new[1],
        router_new[2],
        attn_new[0],
        attn_new[1],
        attn_new[2],
        attn_new[0].astype(jnp.bfloat16),
        up_new[0],
        up_new[1],
        up_new[2],
        up_new[0].astype(jnp.bfloat16),
        down_new[0],
        down_new[1],
        down_new[2],
        down_new[0].astype(jnp.bfloat16),
    )


def solution(mesh):
    return jax.shard_map(
        per_device,
        mesh=mesh,
        in_specs=(
            P(("dp", "expert"), None),
            P(("dp", "expert"), None),
            P("dp", None),
            P("dp"),
            P(None, "dp", None),
            P(None, "dp", None),
            P(),
            P(),
            P(),
            P(),
            P(),
            P(),
            P(),
            P(),
            P(),
            P("expert", "dp", None),
            P("expert", "dp", None),
            P("expert", "dp", None),
            P("expert", "dp", None),
            P("expert", "dp", None),
            P("expert", "dp", None),
            P("expert", "dp", None),
            P("expert", "dp", None),
            P("expert", "dp", None),
        ),
        out_specs=(
            P(("dp", "expert"), None),
            P(("dp", "expert"), None),
            P(),
            P(),
            P(),
            P(),
            P(),
            P(),
            P(),
            P(),
            P(),
            P("expert", "dp", None),
            P("expert", "dp", None),
            P("expert", "dp", None),
            P("expert", "dp", None),
            P("expert", "dp", None),
            P("expert", "dp", None),
            P("expert", "dp", None),
            P("expert", "dp", None),
            P("expert", "dp", None),
            P("expert", "dp", None),
            P("expert", "dp", None),
            P("expert", "dp", None),
        ),
        check_vma=False,
    )
```

profile of v0, /device:TPU:0, one launch (start us, length us, event | category | flops | bytes accessed | tf_op | source)
XLA Modules:
  0.0 1741.3 jit_solution(17309507765780526755)
XLA Ops:
  35.9 10.6 all_gather.52
  48.8 24.5 %gather_fusion.21 = f32[4096]{0:T(1024)S(1)} fusion(f32[1024,8]{0,1:T(8,128)S(1)} %fusion.284, s32[4096]{0:T(1024)S(1)} %reshape.1390), kind=kCustom, calls=%fused_computation.clone | custom fusion | bytes 65536 | tf_op jit(solution)/shard_map/jit(take_along_axis)/gather | solution.py:47
  88.2 8.9 scatter_custom_fusion.1
  97.2 36.1 %reduce-scatter.25.cloned.1.call-done = f32[128,512]{1,0:T(8,128)} async-done(((f32[1024,512]{1,0:T(8,128)}), f32[128,512]{1,0:T(8,128)}) %reduce-scatter.25.cloned.1.call-update) | async-done | bytes 262160 | tf_op jit(solution)/shard_map/reduce_scatter | solution.py:317
  145.8 11.8 all-gather.17.cloned.1.call-done
  159.2 12.5 gather_fusion.22
  177.6 17.2 all-gather.19.cloned.1.call-done
  197.3 35.2 %all-gather.21.cloned.1.call-done = bf16[1,512,2048]{2,1,0:T(8,128)(2,1)} async-done(((bf16[1,128,2048]{2,1,0:T(8,128)(2,1)}), bf16[1,512,2048]{2,1,0:T(8,128)(2,1)}) %all-gather.21.cloned.1.call-update) | async-done | bytes 2097168 | tf_op jit(solution)/shard_map/all_gather | solution.py:131
  241.4 35.2 %reduce-scatter.27.cloned.1.call-done = f32[128,512]{1,0:T(8,128)} async-done(((f32[1024,512]{1,0:T(8,128)}), f32[128,512]{1,0:T(8,128)}) %reduce-scatter.27.cloned.1.call-update) | async-done | bytes 262160 | tf_op jit(solution)/shard_map/reduce_scatter | solution.py:330
  291.4 8.9 all-gather.23.cloned.1.call-done
  301.9 24.5 %gather_fusion.23 = f32[4096]{0:T(1024)S(1)} fusion(f32[1024,8]{0,1:T(8,128)S(1)} %fusion.282, s32[4096]{0:T(1024)S(1)} %reshape.1400), kind=kCustom, calls=%fused_computation.4.clone | custom fusion | bytes 65536 | tf_op jit(solution)/shard_map/jit(take_along_axis)/gather | solution.py:47
  341.2 9.0 scatter_custom_fusion.5
  350.2 35.7 %reduce-scatter.29.cloned.1.call-done = f32[128,512]{1,0:T(8,128)} async-done(((f32[1024,512]{1,0:T(8,128)}), f32[128,512]{1,0:T(8,128)}) %reduce-scatter.29.cloned.1.call-update) | async-done | bytes 262160 | tf_op jit(solution)/shard_map/reduce_scatter | solution.py:317
  395.0 14.4 all-gather.25.cloned.1.call-done
  411.0 12.5 gather_fusion.24
  438.3 34.9 %reduce-scatter.31.cloned.1.call-done = f32[128,512]{1,0:T(8,128)} async-done(((f32[1024,512]{1,0:T(8,128)}), f32[128,512]{1,0:T(8,128)}) %reduce-scatter.31.cloned.1.call-update) | async-done | bytes 262160 | tf_op jit(solution)/shard_map/reduce_scatter | solution.py:330
  487.2 9.6 all-gather.27.cloned.1.call-done
  498.4 24.5 %gather_fusion.25 = f32[4096]{0:T(1024)S(1)} fusion(f32[1024,8]{0,1:T(8,128)S(1)} %fusion.280, s32[4096]{0:T(1024)S(1)} %reshape.1410), kind=kCustom, calls=%fused_computation.5.clone | custom fusion | bytes 65536 | tf_op jit(solution)/shard_map/jit(take_along_axis)/gather | solution.py:47
  537.6 9.1 scatter_custom_fusion.9
  548.8 33.6 %reduce-scatter.33.cloned.1.call-done = f32[128,512]{1,0:T(8,128)} async-done(((f32[1024,512]{1,0:T(8,128)}), f32[128,512]{1,0:T(8,128)}) %reduce-scatter.33.cloned.1.call-update) | async-done | bytes 262160 | tf_op jit(solution)/shard_map/reduce_scatter | solution.py:317
  591.9 20.6 %all-gather.31.cloned.1.call-done = f32[1024,512]{1,0:T(8,128)} async-done(((f32[128,512]{1,0:T(8,128)}), f32[1024,512]{1,0:T(8,128)}) %all-gather.31.cloned.1.call-update) | async-done | bytes 2097168 | tf_op jit(solution)/shard_map/all_gather | solution.py:369
  616.7 18.9 %all-gather.29.cloned.1.call-done = bf16[1024,512]{1,0:T(8,128)(2,1)} async-done(((bf16[128,512]{1,0:T(8,128)(2,1)}), bf16[1024,512]{1,0:T(8,128)(2,1)}) %all-gather.29.cloned.1.call-update) | async-done | bytes 1048592 | tf_op jit(solution)/shard_map/all_gather | solution.py:320
  637.2 12.5 gather_fusion.26
  683.3 10.1 reduce-scatter.39.cloned.1.call-done
  694.6 11.1 scatter_fusion
  705.7 23.9 %reduce-scatter.35.cloned.1.call-done = f32[128,512]{1,0:T(8,128)} async-done(((f32[1024,512]{1,0:T(8,128)}), f32[128,512]{1,0:T(8,128)}) %reduce-scatter.35.cloned.1.call-update) | async-done | bytes 262160 | tf_op jit(solution)/shard_map/reduce_scatter | solution.py:330
  729.6 36.6 %reduce-scatter.37.cloned.1.call-done = f32[128,512]{1,0:T(8,128)} async-done(((f32[1024,512]{1,0:T(8,128)}), f32[128,512]{1,0:T(8,128)}) %reduce-scatter.37.cloned.1.call-update) | async-done | bytes 262160 | tf_op jit(solution)/shard_map/reduce_scatter | solution.py:376
  770.1 28.0 %all-gather.33.cloned.1.call-done = f32[1024,512]{1,0:T(8,128)} async-done(((f32[128,512]{1,0:T(8,128)}), f32[1024,512]{1,0:T(8,128)}) %all-gather.33.cloned.1.call-update) | async-done | bytes 2097168 | tf_op jit(solution)/shard_map/all_gather | solution.py:389
  798.2 5.1 gather_fusion.16
  813.3 5.8 scatter_custom_fusion.15
  827.6 8.6 scatter_custom_fusion.14
  841.7 7.7 reduce-scatter.45.cloned.1.call-done
  850.4 22.1 %scatter_fusion.1 = f32[128,8]{0,1:T(8,128)S(1)} fusion(f32[128,8]{0,1:T(8,128)S(1)} %broadcast_in_dim.271.clone.2, s32[512]{0:T(512)S(1)} %reshape.1284, f32[512]{0:T(512)S(1)} %reshape.1286), kind=kCustom, calls=%fused_computation.58 | custom fusion | flops 512 | bytes 10240 | tf_op jit(solution)/shard_map/transpose(jvp(jit(take_along_axis)))/scatter-add | solution.py:47
  872.8 8.4 reduce-scatter.43.cloned.1.call-done
  881.2 36.3 %reduce-scatter.41.cloned.1.call-done = f32[128,512]{1,0:T(8,128)} async-done(((f32[1024,512]{1,0:T(8,128)}), f32[128,512]{1,0:T(8,128)}) %reduce-scatter.41.cloned.1.call-update) | async-done | bytes 262160 | tf_op jit(solution)/shard_map/reduce_scatter | solution.py:394
  920.9 27.9 %all-gather.35.cloned.1.call-done = f32[1024,512]{1,0:T(8,128)} async-done(((f32[128,512]{1,0:T(8,128)}), f32[1024,512]{1,0:T(8,128)}) %all-gather.35.cloned.1.call-update) | async-done | bytes 2097168 | tf_op jit(solution)/shard_map/all_gather | solution.py:369
  958.2 4.9 fusion.13
  974.9 12.7 reduce-scatter.49.cloned.1.call-done
  988.6 11.1 scatter_fusion.2
  999.8 23.9 %reduce-scatter.47.cloned.1.call-done = f32[128,512]{1,0:T(8,128)} async-done(((f32[1024,512]{1,0:T(8,128)}), f32[128,512]{1,0:T(8,128)}) %reduce-scatter.47.cloned.1.call-update) | async-done | bytes 262160 | tf_op jit(solution)/shard_map/reduce_scatter | solution.py:376
  1026.6 27.9 %all-gather.37.cloned.1.call-done = f32[1024,512]{1,0:T(8,128)} async-done(((f32[128,512]{1,0:T(8,128)}), f32[1024,512]{1,0:T(8,128)}) %all-gather.37.cloned.1.call-update) | async-done | bytes 2097168 | tf_op jit(solution)/shard_map/all_gather | solution.py:389
  1054.6 5.0 gather_fusion.18
  1068.6 5.8 scatter_custom_fusion.19
  1082.5 8.4 scatter_custom_fusion.18
  1094.3 10.4 reduce-scatter.55.cloned.1.call-done
  1105.8 22.1 %scatter_fusion.3 = f32[128,8]{0,1:T(8,128)S(1)} fusion(f32[128,8]{0,1:T(8,128)S(1)} %broadcast_in_dim.271.clone.1, s32[512]{0:T(512)S(1)} %reshape.1296, f32[512]{0:T(512)S(1)} %reshape.1298), kind=kCustom, calls=%fused_computation.60 | custom fusion | flops 512 | bytes 10240 | tf_op jit(solution)/shard_map/transpose(jvp(jit(take_along_axis)))/scatter-add | solution.py:47
  1128.2 8.6 reduce-scatter.53.cloned.1.call-done
  1136.8 36.3 %reduce-scatter.51.cloned.1.call-done = f32[128,512]{1,0:T(8,128)} async-done(((f32[1024,512]{1,0:T(8,128)}), f32[128,512]{1,0:T(8,128)}) %reduce-scatter.51.cloned.1.call-update) | async-done | bytes 262160 | tf_op jit(solution)/shard_map/reduce_scatter | solution.py:394
  1176.3 27.8 %all-gather.39.cloned.1.call-done = f32[1024,512]{1,0:T(8,128)} async-done(((f32[128,512]{1,0:T(8,128)}), f32[1024,512]{1,0:T(8,128)}) %all-gather.39.cloned.1.call-update) | async-done | bytes 2097168 | tf_op jit(solution)/shard_map/all_gather | solution.py:369
  1227.9 15.0 reduce-scatter.59.cloned.1.call-done
  1243.9 11.1 scatter_fusion.4
  1255.1 24.1 %reduce-scatter.57.cloned.1.call-done = f32[128,512]{1,0:T(8,128)} async-done(((f32[1024,512]{1,0:T(8,128)}), f32[128,512]{1,0:T(8,128)}) %reduce-scatter.57.cloned.1.call-update) | async-done | bytes 262160 | tf_op jit(solution)/shard_map/reduce_scatter | solution.py:376
  1282.2 28.0 %all-gather.41.cloned.1.call-done = f32[1024,512]{1,0:T(8,128)} async-done(((f32[128,512]{1,0:T(8,128)}), f32[1024,512]{1,0:T(8,128)}) %all-gather.41.cloned.1.call-update) | async-done | bytes 2097168 | tf_op jit(solution)/shard_map/all_gather | solution.py:389
  1310.2 5.0 gather_fusion.20
  1332.7 5.8 scatter_custom_fusion.23
  1339.2 7.3 add_add_fusion.1
  1373.1 8.3 scatter_custom_fusion.22
  1387.6 22.1 %scatter_fusion.5 = f32[128,8]{0,1:T(8,128)S(1)} fusion(f32[128,8]{0,1:T(8,128)S(1)} %broadcast_in_dim.271, s32[512]{0:T(512)S(1)} %reshape.1308, f32[512]{0:T(512)S(1)} %reshape.1310), kind=kCustom, calls=%fused_computation.62 | custom fusion | flops 512 | bytes 10240 | tf_op jit(solution)/shard_map/transpose(jvp(jit(take_along_axis)))/scatter-add | solution.py:47
  1410.1 30.6 %reduce-scatter.69.cloned.1.call-done = f32[128,2048]{1,0:T(8,128)} async-done(((f32[512,2048]{1,0:T(8,128)}), f32[128,2048]{1,0:T(8,128)}) %reduce-scatter.69.cloned.1.call-update) | async-done | bytes 1048592 | tf_op jit(solution)/shard_map/reduce_scatter | solution.py:414
  1444.8 51.5 %reduce-scatter.71.cloned.1.call-done = f32[128,2048]{1,0:T(8,128)} async-done(((f32[512,2048]{1,0:T(8,128)}), f32[128,2048]{1,0:T(8,128)}) %reduce-scatter.71.cloned.1.call-update) | async-done | bytes 1048592 | tf_op jit(solution)/shard_map/reduce_scatter | solution.py:415
  1500.6 23.1 %reduce-scatter.67.cloned.1.call-done = f32[128,128]{0,1:T(8,128)} async-done(((f32[512,128]{0,1:T(8,128)}), f32[128,128]{0,1:T(8,128)}) %reduce-scatter.67.cloned.1.call-update) | async-done | bytes 65552 | tf_op jit(solution)/shard_map/reduce_scatter | solution.py:413
  1527.7 127.1 %all-reduce.3.cloned.1.call-done = f32[512,128]{1,0:T(8,128)} async-done(((f32[512,128]{1,0:T(8,128)}), f32[512,128]{1,0:T(8,128)}) %all-reduce.3.cloned.1.call-update) | async-done | bytes 262160 | tf_op jit(solution)/shard_map/psum | solution.py:421
  1656.8 35.0 %reduce-scatter.61.cloned.1.call-done = f32[128,512]{1,0:T(8,128)} async-done(((f32[1024,512]{1,0:T(8,128)}), f32[128,512]{1,0:T(8,128)}) %reduce-scatter.61.cloned.1.call-update) | async-done | bytes 262160 | tf_op jit(solution)/shard_map/reduce_scatter | solution.py:394
  1693.5 38.3 %all-reduce = (f32[5,512]{1,0:T(8,128)S(1)}, f32[512,16]{0,1:T(8,128)S(1)}) all-reduce(f32[5,512]{1,0:T(8,128)S(1)} %stack.2, f32[512,16]{0,1:T(8,128)S(1)} %pad_maximum_fusion.3), channel_id=1, replica_groups=mesh['dp'=4,'expert'=8] {'dp','expert'}, use_global_device_ids=true, to_apply=%region_177.182 | all-reduce | flops 10752 | bytes 86016 | tf_op jit(solution)/shard_map/psum | solution.py:421
  (1285 shorter events, 391.5 us)
Async XLA Ops:
  7.2 39.9 %all-gather.15.cloned.1.call-start = ((), (), s32[]{:S(2)}) async-start(), calls=%async_computation.24 | async-start | bytes 1179648 | tf_op jit(solution)/shard_map/all_gather | solution.py:279
  13.8 119.6 %reduce-scatter.25.cloned.1.call-start = ((), (), s32[]{:S(2)}) async-start(), calls=%async_computation.25 | async-start | bytes 2359296 | tf_op jit(solution)/shard_map/reduce_scatter | solution.py:317
  97.1 60.5 %all-gather.17.cloned.1.call-start = ((), (), s32[]{:S(2)}) async-start(), calls=%async_computation.26 | async-start | bytes 1179648 | tf_op jit(solution)/shard_map/all_gather | solution.py:320
  136.6 58.2 %all-gather.19.cloned.1.call-start = ((), (), s32[]{:S(2)}) async-start(), calls=%async_computation.27 | async-start | bytes 2621440 | tf_op jit(solution)/shard_map/all_gather | solution.py:130
  137.6 94.9 %all-gather.21.cloned.1.call-start = ((), (), s32[]{:S(2)}) async-start(), calls=%async_computation.28 | async-start | bytes 2621440 | tf_op jit(solution)/shard_map/all_gather | solution.py:131
  138.5 138.1 %reduce-scatter.27.cloned.1.call-start = ((), (), s32[]{:S(2)}) async-start(), calls=%async_computation.29 | async-start | bytes 2359296 | tf_op jit(solution)/shard_map/reduce_scatter | solution.py:330
  240.7 59.6 %all-gather.23.cloned.1.call-start = ((), (), s32[]{:S(2)}) async-start(), calls=%async_computation.30 | async-start | bytes 1179648 | tf_op jit(solution)/shard_map/all_gather | solution.py:279
  279.4 106.5 %reduce-scatter.29.cloned.1.call-start = ((), (), s32[]{:S(2)}) async-start(), calls=%async_computation.31 | async-start | bytes 2359296 | tf_op jit(solution)/shard_map/reduce_scatter | solution.py:317
  350.2 59.2 %all-gather.25.cloned.1.call-start = ((), (), s32[]{:S(2)}) async-start(), calls=%async_computation.32 | async-start | bytes 1179648 | tf_op jit(solution)/shard_map/all_gather | solution.py:320
  388.5 84.6 %reduce-scatter.31.cloned.1.call-start = ((), (), s32[]{:S(2)}) async-start(), calls=%async_computation.33 | async-start | bytes 2359296 | tf_op jit(solution)/shard_map/reduce_scatter | solution.py:330
  437.5 59.2 %all-gather.27.cloned.1.call-start = ((), (), s32[]{:S(2)}) async-start(), calls=%async_computation.34 | async-start | bytes 1179648 | tf_op jit(solution)/shard_map/all_gather | solution.py:279
  475.8 106.6 %reduce-scatter.33.cloned.1.call-start = ((), (), s32[]{:S(2)}) async-start(), calls=%async_computation.35 | async-start | bytes 2359296 | tf_op jit(solution)/shard_map/reduce_scatter | solution.py:317
  546.8 65.7 %all-gather.31.cloned.1.call-start = ((), (), s32[]{:S(2)}) async-start(), calls=%async_computation.38 | async-start | bytes 2359296 | tf_op jit(solution)/shard_map/all_gather | solution.py:369
  548.8 86.8 %all-gather.29.cloned.1.call-start = ((), (), s32[]{:S(2)}) async-start(), calls=%async_computation.36 | async-start | bytes 1179648 | tf_op jit(solution)/shard_map/all_gather | solution.py:320
  585.0 108.5 %reduce-scatter.39.cloned.1.call-start = ((), (), s32[]{:S(2)}) async-start(), calls=%async_computation.40 | async-start | bytes 36864 | tf_op jit(solution)/shard_map/reduce_scatter | solution.py:377
  663.7 66.0 %reduce-scatter.35.cloned.1.call-start = ((), (), s32[]{:S(2)}) async-start(), calls=%async_computation.37 | async-start | bytes 2359296 | tf_op jit(solution)/shard_map/reduce_scatter | solution.py:330
  668.9 97.3 %reduce-scatter.37.cloned.1.call-start = ((), (), s32[]{:S(2)}) async-start(), calls=%async_computation.39 | async-start | bytes 2359296 | tf_op jit(solution)/shard_map/reduce_scatter | solution.py:376
  680.3 117.9 %all-gather.33.cloned.1.call-start = ((), (), s32[]{:S(2)}) async-start(), calls=%async_computation.41 | async-start | bytes 2359296 | tf_op jit(solution)/shard_map/all_gather | solution.py:389
  705.7 97.5 %copy-start = (f32[128,8]{0,1:T(8,128)}, f32[128,8]{0,1:T(8,128)S(1)}, u32[]{:S(2)}) copy-start(f32[128,8]{0,1:T(8,128)S(1)} %scatter_fusion) | copy-start | bytes 12292
  770.1 79.3 %reduce-scatter.45.cloned.1.call-start = ((), (), s32[]{:S(2)}) async-start(), calls=%async_computation.44 | async-start | bytes 36864 | tf_op jit(solution)/shard_map/reduce_scatter | solution.py:396
  819.8 61.5 %reduce-scatter.43.cloned.1.call-start = ((), (), s32[]{:S(2)}) async-start(), calls=%async_computation.43 | async-start | bytes 589824 | tf_op jit(solution)/shard_map/reduce_scatter | solution.py:395
  824.5 93.0 %reduce-scatter.41.cloned.1.call-start = ((), (), s32[]{:S(2)}) async-start(), calls=%async_computation.42 | async-start | bytes 2359296 | tf_op jit(solution)/shard_map/reduce_scatter | solution.py:394
  836.2 112.5 %all-gather.35.cloned.1.call-start = ((), (), s32[]{:S(2)}) async-start(), calls=%async_computation.45 | async-start | bytes 2359296 | tf_op jit(solution)/shard_map/all_gather | solution.py:369
  920.8 66.7 %reduce-scatter.49.cloned.1.call-start = ((), (), s32[]{:S(2)}) async-start(), calls=%async_computation.47 | async-start | bytes 36864 | tf_op jit(solution)/shard_map/reduce_scatter | solution.py:377
  957.9 65.7 %reduce-scatter.47.cloned.1.call-start = ((), (), s32[]{:S(2)}) async-start(), calls=%async_computation.46 | async-start | bytes 2359296 | tf_op jit(solution)/shard_map/reduce_scatter | solution.py:376
  970.6 84.0 %all-gather.37.cloned.1.call-start = ((), (), s32[]{:S(2)}) async-start(), calls=%async_computation.48 | async-start | bytes 2359296 | tf_op jit(solution)/shard_map/all_gather | solution.py:389
  1026.6 78.2 %reduce-scatter.55.cloned.1.call-start = ((), (), s32[]{:S(2)}) async-start(), calls=%async_computation.51 | async-start | bytes 36864 | tf_op jit(solution)/shard_map/reduce_scatter | solution.py:396
  1075.1 61.7 %reduce-scatter.53.cloned.1.call-start = ((), (), s32[]{:S(2)}) async-start(), calls=%async_computation.50 | async-start | bytes 589824 | tf_op jit(solution)/shard_map/reduce_scatter | solution.py:395
  1079.8 93.2 %reduce-scatter.51.cloned.1.call-start = ((), (), s32[]{:S(2)}) async-start(), calls=%async_computation.49 | async-start | bytes 2359296 | tf_op jit(solution)/shard_map/reduce_scatter | solution.py:394
  1090.9 113.2 %all-gather.39.cloned.1.call-start = ((), (), s32[]{:S(2)}) async-start(), calls=%async_computation.52 | async-start | bytes 2359296 | tf_op jit(solution)/shard_map/all_gather | solution.py:369
  1176.3 66.6 %reduce-scatter.59.cloned.1.call-start = ((), (), s32[]{:S(2)}) async-start(), calls=%async_computation.54 | async-start | bytes 36864 | tf_op jit(solution)/shard_map/reduce_scatter | solution.py:377
  1213.2 66.0 %reduce-scatter.57.cloned.1.call-start = ((), (), s32[]{:S(2)}) async-start(), calls=%async_computation.53 | async-start | bytes 2359296 | tf_op jit(solution)/shard_map/reduce_scatter | solution.py:376
  1225.5 84.7 %all-gather.41.cloned.1.call-start = ((), (), s32[]{:S(2)}) async-start(), calls=%async_computation.55 | async-start | bytes 2359296 | tf_op jit(solution)/shard_map/all_gather | solution.py:389
  1282.2 88.2 %reduce-scatter.63.cloned.1.call-start = ((), (), s32[]{:S(2)}) async-start(), calls=%async_computation.57 | async-start | bytes 589824 | tf_op jit(solution)/shard_map/reduce_scatter | solution.py:395
  1324.9 61.7 %reduce-scatter.65.cloned.1.call-start = ((), (), s32[]{:S(2)}) async-start(), calls=%async_computation.58 | async-start | bytes 36864 | tf_op jit(solution)/shard_map/reduce_scatter | solution.py:396
  1339.2 101.5 %reduce-scatter.69.cloned.1.call-start = ((), (), s32[]{:S(2)}) async-start(), calls=%async_computation.61 | async-start | bytes 5242880 | tf_op jit(solution)/shard_map/reduce_scatter | solution.py:414
  1346.5 149.7 %reduce-scatter.71.cloned.1.call-start = ((), (), s32[]{:S(2)}) async-start(), calls=%async_computation.62 | async-start | bytes 5242880 | tf_op jit(solution)/shard_map/reduce_scatter | solution.py:415
  1356.5 167.3 %reduce-scatter.67.cloned.1.call-start = ((), (), s32[]{:S(2)}) async-start(), calls=%async_computation.60 | async-start | bytes 327680 | tf_op jit(solution)/shard_map/reduce_scatter | solution.py:413
  1369.9 285.0 %all-reduce.3.cloned.1.call-start = ((), (), s32[]{:S(2)}) async-start(), calls=%async_computation.59 | async-start | bytes 524288 | tf_op jit(solution)/shard_map/psum | solution.py:421
  1372.2 319.6 %reduce-scatter.61.cloned.1.call-start = ((), (), s32[]{:S(2)}) async-start(), calls=%async_computation.56 | async-start | bytes 2359296 | tf_op jit(solution)/shard_map/reduce_scatter | solution.py:394
  1444.7 210.1 %copy-start.141 = (f32[512,128]{1,0:T(8,128)S(1)}, f32[512,128]{1,0:T(8,128)}, u32[]{:S(2)}) copy-start(f32[512,128]{1,0:T(8,128)} %param.42) | copy-start | bytes 786436
  1444.7 210.1 %copy-start.165 = (f32[512,128]{1,0:T(8,128)S(1)}, f32[512,128]{1,0:T(8,128)}, u32[]{:S(2)}) copy-start(f32[512,128]{1,0:T(8,128)} %param.43) | copy-start | bytes 786436
  1444.8 210.1 %copy-start.166 = (f32[512,128]{1,0:T(8,128)S(1)}, f32[512,128]{1,0:T(8,128)}, u32[]{:S(2)}) copy-start(f32[512,128]{1,0:T(8,128)} %param.44) | copy-start | bytes 786436
  1500.5 191.3 %copy-start.65 = (bf16[128,512]{1,0:T(8,128)(2,1)S(1)}, bf16[128,512]{1,0:T(8,128)(2,1)}, u32[]{:S(2)}) copy-start(bf16[128,512]{1,0:T(8,128)(2,1)} %param.33) | copy-start | bytes 393220
  1500.5 191.3 %copy-start.72 = (bf16[512,128]{1,0:T(8,128)(2,1)S(1)}, bf16[512,128]{1,0:T(8,128)(2,1)}, u32[]{:S(2)}) copy-start(bf16[512,128]{1,0:T(8,128)(2,1)} %convert_element_type.304) | copy-start | bytes 393220
  1500.5 191.3 %copy-start.174 = (f32[128,128]{0,1:T(8,128)S(1)}, f32[128,128]{0,1:T(8,128)}, u32[]{:S(2)}) copy-start(f32[128,128]{0,1:T(8,128)} %reduce-scatter.63.cloned.1.call-done) | copy-start | bytes 196612
  1500.6 191.3 %copy-start.179 = (f32[1,512]{1,0:T(1,128)S(1)}, f32[1,512]{1,0:T(1,128)}, u32[]{:S(2)}) copy-start(f32[1,512]{1,0:T(1,128)} %copy-done.175) | copy-start | bytes 6148
  1500.6 191.2 %copy-start.257 = (f32[128]{0:T(128)S(1)}, f32[128]{0:T(128)}, u32[]{:S(2)}) copy-start(f32[128]{0:T(128)} %copy-done.256) | copy-start | bytes 1540
  1500.6 192.5 %copy-start.344 = (f32[128]{0:T(128)S(1)}, f32[128]{0:T(128)}, u32[]{:S(2)}) copy-start(f32[128]{0:T(128)} %copy-done.343) | copy-start | bytes 1540
  1500.6 192.5 %copy-start.310 = (f32[128]{0:T(128)S(1)}, f32[128]{0:T(128)}, u32[]{:S(2)}) copy-start(f32[128]{0:T(128)} %copy-done.309) | copy-start | bytes 1540
  1500.6 192.8 %copy-start.269 = (f32[512]{0:T(512)S(1)}, f32[512]{0:T(512)}, u32[]{:S(2)}) copy-start(f32[512]{0:T(512)} %get-tuple-element.374) | copy-start | bytes 6148
  1500.6 192.8 %copy-start.273 = (f32[512]{0:T(512)S(1)}, f32[512]{0:T(512)}, u32[]{:S(2)}) copy-start(f32[512]{0:T(512)} %get-tuple-element.372) | copy-start | bytes 6148
  1500.6 192.8 %copy-start.268 = (f32[512]{0:T(512)S(1)}, f32[512]{0:T(512)}, u32[]{:S(2)}) copy-start(f32[512]{0:T(512)} %get-tuple-element.383) | copy-start | bytes 6148
  1500.6 192.8 %copy-start.272 = (f32[512]{0:T(512)S(1)}, f32[512]{0:T(512)}, u32[]{:S(2)}) copy-start(f32[512]{0:T(512)} %get-tuple-element.381) | copy-start | bytes 6148
  1524.7 207.1 %copy-start.109 = (f32[128,512]{1,0:T(8,128)S(1)}, f32[128,512]{1,0:T(8,128)}, u32[]{:S(2)}) copy-start(f32[128,512]{1,0:T(8,128)} %add_add_fusion.9) | copy-start | bytes 786436
  1524.7 207.1 %copy-start.144 = (f32[128,512]{1,0:T(8,128)S(1)}, f32[128,512]{1,0:T(8,128)}, u32[]{:S(2)}) copy-start(f32[128,512]{1,0:T(8,128)} %get-tuple-element.438) | copy-start | bytes 786436
  1524.7 207.1 %copy-start.331 = (f32[128]{0:T(128)S(1)}, f32[128]{0:T(128)}, u32[]{:S(2)}) copy-start(f32[128]{0:T(128)} %get-tuple-element.425) | copy-start | bytes 1540
  1527.6 205.0 %copy-start.184 = (f32[512,16]{0,1:T(8,128)S(1)}, f32[512,16]{0,1:T(8,128)}, u32[]{:S(2)}) copy-start(f32[512,16]{0,1:T(8,128)} %param.45) | copy-start | bytes 98308
  1527.6 205.0 %copy-start.227 = (f32[512,16]{0,1:T(8,128)S(1)}, f32[512,16]{0,1:T(8,128)}, u32[]{:S(2)}) copy-start(f32[512,16]{0,1:T(8,128)} %param.46) | copy-start | bytes 98308
  1527.6 205.0 %copy-start.228 = (f32[512,16]{0,1:T(8,128)S(1)}, f32[512,16]{0,1:T(8,128)}, u32[]{:S(2)}) copy-start(f32[512,16]{0,1:T(8,128)} %param.47) | copy-start | bytes 98308
  1527.6 205.7 %copy-start.218 = (f32[5,512]{1,0:T(8,128)S(1)}, f32[5,512]{1,0:T(8,128)}, u32[]{:S(2)}) copy-start(f32[5,512]{1,0:T(8,128)} %param.39) | copy-start | bytes 30724
  1527.6 205.7 %copy-start.249 = (f32[5,512]{1,0:T(8,128)S(1)}, f32[5,512]{1,0:T(8,128)}, u32[]{:S(2)}) copy-start(f32[5,512]{1,0:T(8,128)} %param.40) | copy-start | bytes 30724
  1527.7 205.7 %copy-start.250 = (f32[5,512]{1,0:T(8,128)S(1)}, f32[5,512]{1,0:T(8,128)}, u32[]{:S(2)}) copy-start(f32[5,512]{1,0:T(8,128)} %param.41) | copy-start | bytes 30724
  1527.7 205.7 %copy-start.342 = (f32[5]{0:T(128)S(1)}, f32[5]{0:T(128)}, u32[]{:S(2)}) copy-start(f32[5]{0:T(128)} %constant.398.clone) | copy-start | bytes 64
  (334 other events, 6364.5 us)
Sparse Core Ops, SparseCore 0:
  13.9 24.8 all-gather.14
  97.2 36.0 reduce-scatter.24
  136.7 20.8 all-gather.16
  159.9 34.9 all-gather.18
  197.1 35.2 all-gather.20
  240.9 35.7 reduce-scatter.26
  279.5 20.7 all-gather.22
  350.3 35.5 reduce-scatter.28
  388.6 20.7 all-gather.24
  437.7 35.4 reduce-scatter.30
  475.9 20.7 all-gather.26
  546.9 35.4 reduce-scatter.32
  584.6 27.8 all-gather.30
  613.9 21.5 all-gather.28
  663.8 29.6 reduce-scatter.38
  695.7 33.8 reduce-scatter.34
  731.9 34.3 reduce-scatter.36
  770.2 27.8 all-gather.32
  819.9 29.4 reduce-scatter.44
  852.1 29.1 reduce-scatter.42
  883.6 33.8 reduce-scatter.40
  920.9 27.8 all-gather.34
  958.0 29.4 reduce-scatter.48
  989.7 33.9 reduce-scatter.46
  1026.7 27.8 all-gather.36
  1075.2 29.5 reduce-scatter.54
  1107.5 29.1 reduce-scatter.52
  1139.1 33.9 reduce-scatter.50
  1176.4 27.6 all-gather.38
  1213.3 29.5 reduce-scatter.58
  1245.3 33.9 reduce-scatter.56
  1282.3 27.8 all-gather.40
  1325.0 30.4 reduce-scatter.62
  1358.3 28.2 reduce-scatter.64
  1389.8 50.8 reduce-scatter.68
  1443.5 52.6 reduce-scatter.70
  1499.6 24.0 reduce-scatter.66
  1529.8 124.9 all-reduce.2
  1657.0 34.7 reduce-scatter.60
where the time goes:
time: 1750 us; the launch traced here: 1740 us
  waiting for transfers between devices  978 us (56%)
  other arithmetic  305 us (17%)
  local copies, waits for them, and re-layouts  274 us (16%)
  matrix products  112 us (6%)
  blocking collectives  48.9 us (3%)
  between operations  20.4 us (1%)
    gather x60, local copies, waits for them, and re-layouts, dense_gates(): picked = jnp.take_along_axis(logits, chosen, axis=1)  133 us
    psum x1, waiting for transfers between devices, per_device(): lax.psum((shared_part, kv_acc, router_part), ('dp', 'expert'))  127 us
    reduce_scatter x3, waiting for transfers between devices, per_device(): lax.psum_scatter(attn_in_part, 'expert', scatter_dimension=0, tiled=True)  108 us
    reduce_scatter x3, waiting for transfers between devices, per_device(): mixed = lax.psum_scatter(contrib, 'expert', scatter_dimension=0, tiled=True)  105 us
    scatter-add x16, other arithmetic, dense_gates(): picked = jnp.take_along_axis(logits, chosen, axis=1)  104 us
    reduce_scatter x3, waiting for transfers between devices, per_device(): lax.psum_scatter(ffn_contrib, 'expert', scatter_dimension=0, tiled=True)  93.9 us
    reduce_scatter x3, waiting for transfers between devices, per_device(): lax.psum_scatter(ffn_in_part, 'expert', scatter_dimension=0, tiled=True)  84.6 us
    all_gather x3, waiting for transfers between devices, per_device(): attn_grad_all = lax.all_gather(middle_grad, 'expert', axis=0, tiled=True)  83.9 us
  transfers between devices with their start and end apart: 39, of which 37 were waited for; matrix products, arithmetic and copies ran while one was open for 20% of the time, Pallas kernels for 0%

commit v1 on v0

v1 whole, which is shorter than its diff:
```python
import functools
import math

import jax
import jax.numpy as jnp
from jax import lax
from jax.experimental import pallas as pl
from jax.experimental.pallas import tpu as pltpu
from jax.sharding import PartitionSpec as P

D = 512
HD = 64
FF = 2048
KATT = 4
KFF = 2
LOOPS = 3
STEP = 10
MAXLEN = 512
FILLED = 896

ln_eps = 1e-05
beta_one = 0.9
beta_two = 0.999
adam_eps = 1e-08
decay_rate = 0.01
masked_score = -1e30

F32 = jnp.float32
BF16 = jnp.bfloat16
MESH = pl.DeviceIdType.MESH
LANES = 128
RANK_LANE = 16
RUN_LANE = 17
SEG_LANE = 18
TILE = 512
EXTRA = 16


def nn(left, right):
    return lax.dot_general(left, right, (((1,), (0,)), ((), ())), preferred_element_type=F32)


def nt(left, right):
    return lax.dot_general(left, right, (((1,), (1,)), ((), ())), preferred_element_type=F32)


def tn(left, right):
    return lax.dot_general(left, right, (((0,), (0,)), ((), ())), preferred_element_type=F32)


def normalise(values):
    centre = values - jnp.mean(values, axis=-1, keepdims=True)
    inverse = lax.rsqrt(jnp.mean(centre * centre, axis=-1, keepdims=True) + ln_eps)
    return centre * inverse, inverse


def norm_back(grad, unit, inverse, gain):
    scaled = grad * gain
    first = jnp.mean(scaled, axis=-1, keepdims=True)
    second = jnp.mean(scaled * unit, axis=-1, keepdims=True)
    return inverse * (scaled - first - unit * second)


def masked_softmax(logits, valid):
    top = jnp.max(jnp.where(valid, logits, masked_score), axis=-1, keepdims=True)
    powers = jnp.where(valid, jnp.exp(jnp.where(valid, logits - top, 0.0)), 0.0)
    return powers / jnp.maximum(jnp.sum(powers, axis=-1, keepdims=True), 0.5)


def adam_update(weight, moment, second, grad, rate, decay):
    moment_new = beta_one * moment + (1.0 - beta_one) * grad
    second_new = beta_two * second + (1.0 - beta_two) * grad * grad
    moment_hat = moment_new / (1.0 - beta_one**STEP)
    second_hat = second_new / (1.0 - beta_two**STEP)
    weight_new = weight - rate * (moment_hat / (jnp.sqrt(second_hat) + adam_eps) + decay * weight)
    return (weight_new, moment_new, second_new)


def block_kernel(
    n_exp,
    n_dp,
    n_act,
    cap,
    x_ref,
    cot_ref,
    meta_ref,
    rowm_ref,
    vec_ref,
    kvw_ref,
    rw_ref,
    aw_ref,
    uw_ref,
    dw_ref,
    out_ref,
    xgrad_ref,
    ugrad_ref,
    dgrad_ref,
    agrad_ref,
    small_ref,
    kvb,
    rb,
    w_all,
    up_w,
    down_w,
    up_acc,
    down_acc,
    attn_acc,
    small_acc,
    state,
    middle,
    normed_k,
    second_k,
    kv_k,
    q_k,
    o_k,
    p_k,
    bias,
    mix,
    dga,
    dkv_t,
    dkv,
    gate_k,
    rows_all,
    rows_k,
    hid,
    gprime,
    part_k,
    fgate_k,
    sgrad,
    carry,
    total,
    pair_send,
    pair_recv,
    far_send,
    far_recv,
    dkv_send,
    dkv_recv,
    ug_recv,
    dg_recv,
    a_pair_send,
    a_pair_recv,
    a_far_send,
    a_far_recv,
    a_total,
    a_stage,
    a_recv,
    s_pair_send,
    s_pair_recv,
    s_far_send,
    s_far_recv,
    s_total,
    s_dp,
    s_all,
    w_send,
    w_recv,
    ag_send,
    ag_recv,
    kg_send,
    kg_recv,
    wg_send,
    wg_recv,
    sg_send,
    sg_recv,
    rs_sems,
    s_sems,
    a_sems,
    dk_send,
    dk_recv,
    g_send,
    g_recv,
    t_send,
    t_recv,
):
    me = lax.axis_index("expert")
    dp = lax.axis_index("dp")
    pairs = n_exp // 2
    core = lax.rem(me, 2)
    chip = lax.div(me, 2)
    sibling = 2 * chip + 1 - core
    own = x_ref.shape[0]
    width = x_ref.shape[1]
    shard = aw_ref.shape[0]
    valid_rows = n_act * own
    window = min(n_act, MAXLEN // own + 1)
    keys = window * own
    win_at = jnp.clip(me - (window - 1), 0, n_act - window)
    scale = HD ** (-0.5)
    active = me < n_act

    def to_expert(src, dst, send, recv, where):
        return pltpu.make_async_remote_copy(
            src_ref=src,
            dst_ref=dst,
            send_sem=send,
            recv_sem=recv,
            device_id={"expert": where},
            device_id_type=MESH,
        )

    def to_dp(src, dst, send, recv, where):
        return pltpu.make_async_remote_copy(
            src_ref=src,
            dst_ref=dst,
            send_sem=send,
            recv_sem=recv,
            device_id={"dp": where},
            device_id_type=MESH,
        )

    def each_peer(body):
        def step(k, none):
            body(lax.rem(dp + k, n_dp))
            return none

        lax.fori_loop(1, n_dp, step, 0)

    def gather_start(buf, send, recv, count):
        @pl.when(me < count)
        def _():
            for k in range(1, pairs):
                zz = lax.rem(chip + k, pairs)
                to_expert(buf.at[me], buf.at[me], send.at[zz], recv.at[me], 2 * zz + core).start()
            to_expert(buf.at[me], buf.at[me], send.at[chip], recv.at[me], sibling).start()

    def gather_finish(buf, send, recv, count):
        for k in range(1, pairs):
            zz = lax.rem(chip + k, pairs)
            src = 2 * zz + core

            @pl.when(src < count)
            def _():
                to_expert(buf.at[src], buf.at[src], send.at[zz], recv.at[src], src).wait_recv()
                to_expert(
                    buf.at[src], buf.at[src], send.at[pairs + zz], recv.at[src], sibling
                ).start()

        for k in range(pairs):
            zz = lax.rem(chip + k, pairs)
            src = 2 * zz + 1 - core

            @pl.when(src < count)
            def _():
                to_expert(buf.at[src], buf.at[src], send.at[zz], recv.at[src], sibling).wait_recv()

        @pl.when(me < count)
        def _():
            for k in range(1, pairs):
                zz = lax.rem(chip + k, pairs)
                to_expert(
                    buf.at[me], buf.at[me], send.at[zz], recv.at[me], 2 * zz + core
                ).wait_send()
            to_expert(buf.at[me], buf.at[me], send.at[chip], recv.at[me], sibling).wait_send()

        for k in range(1, pairs):
            zz = lax.rem(chip + k, pairs)
            src = 2 * zz + core

            @pl.when(src < count)
            def _():
                to_expert(
                    buf.at[src], buf.at[src], send.at[pairs + zz], recv.at[src], sibling
                ).wait_send()

    def reduce_blocks(make, count, rows, psend, precv, fsend, frecv, sems, result):
        part = pl.ds(0, rows)
        rs_psend, rs_precv, rs_fsend, rs_frecv = (sems.at[index] for index in range(4))

        def pair_copy(zz):
            return to_expert(
                psend.at[zz, part],
                precv.at[zz, part],
                rs_psend.at[zz],
                rs_precv.at[zz],
                sibling,
            )

        def far_copy(zz, slot):
            return to_expert(
                fsend.at[zz, part],
                frecv.at[slot, part],
                rs_fsend.at[zz],
                rs_frecv.at[slot],
                2 * zz + core,
            )

        for k in range(pairs):
            zz = lax.rem(chip + 1 + k, pairs)
            block = 2 * zz + 1 - core

            @pl.when(block < count)
            def _():
                psend[zz, part] = make(block).astype(BF16)
                pair_copy(zz).start()

        for k in range(1, pairs):
            zz = lax.rem(chip + k, pairs)
            block = 2 * zz + core

            @pl.when(block < count)
            def _():
                mine = make(block)
                pair_copy(zz).wait_recv()
                fsend[zz, part] = (mine + precv[zz, part].astype(F32)).astype(BF16)
                far_copy(zz, chip).start()

        @pl.when(me < count)
        def _():
            mine = make(me)
            pair_copy(chip).wait_recv()
            result[part] = mine + precv[chip, part].astype(F32)
            for k in range(1, pairs):
                zz = lax.rem(chip + k, pairs)
                far_copy(zz, zz).wait_recv()
                result[part] += frecv[zz, part].astype(F32)

        @pl.when(me >= count)
        def _():
            result[part] = jnp.zeros((rows, result.shape[1]), F32)

        for k in range(pairs):
            zz = lax.rem(chip + 1 + k, pairs)

            @pl.when(2 * zz + 1 - core < count)
            def _():
                pair_copy(zz).wait_send()

        for k in range(1, pairs):
            zz = lax.rem(chip + k, pairs)

            @pl.when(2 * zz + core < count)
            def _():
                far_copy(zz, chip).wait_send()

    barrier = pltpu.get_barrier_semaphore()
    for k in range(1, n_exp):
        pl.semaphore_signal(
            barrier, inc=1, device_id={"expert": lax.rem(me + k, n_exp)}, device_id_type=MESH
        )
    for k in range(1, n_dp):
        pl.semaphore_signal(
            barrier, inc=1, device_id={"dp": lax.rem(dp + k, n_dp)}, device_id_type=MESH
        )
    dp_rows = pl.ds(pl.multiple_of(dp * shard, shard), shard)
    w_all[me, dp_rows] = aw_ref[...].astype(BF16)
    up_w[dp_rows] = uw_ref[...].astype(BF16)
    down_w[dp_rows] = dw_ref[...].astype(BF16)
    pl.semaphore_wait(barrier, n_exp + n_dp - 2)

    def weight_copy(index, peer, slot):
        rows = pl.ds(pl.multiple_of(slot * shard, shard), shard)
        ref = (w_all.at[me], up_w, down_w)[index].at[rows]
        return to_dp(ref, ref, w_send.at[index, peer], w_recv.at[index, slot], peer)

    for index in range(3):
        each_peer(lambda peer, index=index: weight_copy(index, peer, dp).start())

    kvb[...] = kvw_ref[...].astype(BF16)
    rb[...] = rw_ref[...].astype(BF16)
    gain_one = vec_ref[0:1, :]
    bias_one = vec_ref[1:2, :]
    gain_two = vec_ref[2:3, :]
    bias_two = vec_ref[3:4, :]
    halt = vec_ref[4:5, :]
    state[0] = x_ref[...].astype(F32)
    own_rows = pl.ds(pl.multiple_of(me * own, own), own)
    seg_own = meta_ref[0, own_rows, SEG_LANE : SEG_LANE + 1]
    key_cols = pl.ds(pl.multiple_of(win_at * own, own), keys)
    seg_keys = rowm_ref[LOOPS, :, key_cols]
    row_at = me * own + lax.broadcasted_iota(jnp.int32, (own, keys), 0)
    key_at = win_at * own + lax.broadcasted_iota(jnp.int32, (own, keys), 1)
    allowed = (seg_own == seg_keys) & (key_at <= row_at)
    bias[...] = jnp.where(allowed, 0.0, masked_score)
    up_acc[...] = jnp.zeros_like(up_acc)
    down_acc[...] = jnp.zeros_like(down_acc)
    attn_acc[...] = jnp.zeros_like(attn_acc)
    small_acc[...] = jnp.zeros_like(small_acc)

    each_peer(lambda peer: weight_copy(0, peer, peer).wait_recv())
    gather_start(w_all, wg_send, wg_recv, n_exp)
    gather_finish(w_all, wg_send, wg_recv, n_exp)

    lane = lax.broadcasted_iota(jnp.int32, (own, LANES), 1)
    lane_two = lax.broadcasted_iota(jnp.int32, (2 * own, LANES), 1)
    lane_cap = lax.broadcasted_iota(jnp.int32, (cap, LANES), 1)
    slot_rows = lax.broadcasted_iota(jnp.int32, (cap, valid_rows), 0).astype(F32)
    slot_cols = lax.broadcasted_iota(jnp.int32, (own, cap), 1).astype(F32)

    def gather_matrix(loop):
        ranks = rowm_ref[loop, :, 0:valid_rows]
        return jnp.where(slot_rows == ranks, 1.0, 0.0).astype(BF16)

    def scatter_matrix(loop, block):
        rows = pl.ds(pl.multiple_of(block * own, own), own)
        ranks = meta_ref[loop, rows, RANK_LANE : RANK_LANE + 1]
        return jnp.where(slot_cols == ranks, 1.0, 0.0).astype(BF16)

    def column(values, index, lanes):
        return jnp.sum(jnp.where(lanes == index, values, 0.0), axis=1, keepdims=True)

    def cap_rows(loop):
        return pl.ds(pl.multiple_of(loop * cap, cap), cap)

    def window_keys(loop):
        return kv_k[loop, pl.ds(win_at, window)].reshape(keys, 2 * HD)

    def forward(loop, none):
        current = state[loop]
        unit, _ = normalise(current)
        normed = (unit * gain_one + bias_one).astype(BF16)
        normed_k[loop] = normed
        kv_k[loop, me] = nn(normed, kvb[...]).astype(BF16)
        gather_start(kv_k.at[loop], kg_send, kg_recv, n_act)
        info = meta_ref[loop, own_rows]
        running = info[:, RUN_LANE : RUN_LANE + 1]
        gates = masked_softmax(nn(normed, rb[...]), (info > 0.5) & (lane < n_exp))
        gate_k[loop] = gates

        def queries(expert, none):
            query = jnp.where(lane < HD, nn(normed, w_all[expert]), 0.0).astype(BF16)
            q_k[loop, pl.ds(pl.multiple_of(expert * own, own), own)] = query
            return none

        lax.fori_loop(0, n_exp, queries, 0)
        gather_finish(kv_k.at[loop], kg_send, kg_recv, n_act)
        kv_rows = window_keys(loop)
        mix[...] = jnp.zeros_like(mix)

        def attend(pair, none):
            rows = pl.ds(pl.multiple_of(pair * 2 * own, 2 * own), 2 * own)
            scores = nt(q_k[loop, rows], kv_rows) * scale
            scores = (scores.reshape(2, own, keys) + bias[...][None]).reshape(2 * own, keys)
            powers = jnp.exp(scores - jnp.max(scores, axis=1, keepdims=True))
            prob = (powers * (1.0 / jnp.sum(powers, axis=1, keepdims=True))).astype(BF16)
            p_k[loop, rows] = prob
            outs = jnp.where(lane_two < HD, 0.0, nn(prob, kv_rows)).astype(BF16)
            o_k[loop, rows] = outs
            for half in range(2):
                expert = 2 * pair + half
                gate = column(gates, expert, lane) * running
                mix[...] += gate * nt(outs[half * own : (half + 1) * own], w_all[expert])
            return none

        lax.fori_loop(0, n_exp // 2, attend, 0)
        centre = current + mix[...]
        middle[loop] = centre
        unit, _ = normalise(centre)
        second = (unit * gain_two + bias_two).astype(BF16)
        second_k[loop] = second
        rows_all[me] = second
        gather_start(rows_all, ag_send, ag_recv, n_act)

        @pl.when(loop == 0)
        def _():
            for index in (1, 2):
                each_peer(lambda peer, index=index: weight_copy(index, peer, peer).wait_recv())

        gather_finish(rows_all, ag_send, ag_recv, n_act)
        places = gather_matrix(loop)
        rows_in = nn(places, rows_all[0:n_act].reshape(valid_rows, width)).astype(BF16)
        rows_k[cap_rows(loop)] = rows_in
        chosen = nn(places, meta_ref[loop, 0:valid_rows].astype(BF16))
        allowed_lanes = (chosen > 0.5) & (lane_cap >= n_exp) & (lane_cap < 2 * n_exp)
        gate = column(masked_softmax(nn(rows_in, rb[...]), allowed_lanes), n_exp + me, lane_cap)
        fgate_k[cap_rows(loop)] = gate
        part_k[cap_rows(loop)] = jnp.zeros((cap, width), F32)

        def hidden_tile(tile, none):
            cols = pl.ds(pl.multiple_of(tile * TILE, TILE), TILE)
            inner = nn(rows_in, up_w[:, cols])
            root = math.sqrt(2.0 / math.pi)
            square = inner * inner
            curve = jnp.tanh(root * inner * (1.0 + 0.044715 * square))
            upper = 0.5 * (1.0 + curve)
            hidden = (inner * upper).astype(BF16)
            slope = upper + 0.5 * inner * (1.0 - curve * curve) * (
                root + (3.0 * 0.044715 * root) * square
            )
            hid[cap_rows(loop), cols] = hidden
            gprime[cap_rows(loop), cols] = slope.astype(BF16)
            part_k[cap_rows(loop)] += nt(hidden, down_w[:, cols])
            return none

        lax.fori_loop(0, up_w.shape[1] // TILE, hidden_tile, 0)
        terms = (part_k[cap_rows(loop)] * gate).astype(BF16)
        reduce_blocks(
            lambda block: nn(scatter_matrix(loop, block), terms),
            n_act,
            own,
            pair_send,
            pair_recv,
            far_send,
            far_recv,
            rs_sems,
            total,
        )
        state[loop + 1] = jnp.where(running > 0.5, centre + total[0:own], current)
        return none

    lax.fori_loop(0, LOOPS, forward, 0)

    cot = cot_ref[...].astype(F32)
    first, next_one, last = state[1], state[2], state[3]
    chance_one = jax.nn.sigmoid(jnp.sum(first * halt, axis=1, keepdims=True))
    chance_two = jax.nn.sigmoid(jnp.sum(next_one * halt, axis=1, keepdims=True))
    stay = 1.0 - chance_one
    weight_two = stay * chance_two
    weight_three = stay * (1.0 - chance_two)
    out_ref[...] = chance_one * first + weight_two * next_one + weight_three * last
    dot_one = jnp.sum(cot * first, axis=1, keepdims=True)
    dot_two = jnp.sum(cot * next_one, axis=1, keepdims=True)
    dot_three = jnp.sum(cot * last, axis=1, keepdims=True)
    slope_one = (chance_one * stay) * (
        dot_one - chance_two * dot_two - (1.0 - chance_two) * dot_three
    )
    slope_two = (chance_two * (1.0 - chance_two)) * stay * (dot_two - dot_three)
    sgrad[0] = chance_one * cot + slope_one * halt
    sgrad[1] = weight_two * cot + slope_two * halt
    sgrad[2] = weight_three * cot
    vec_at = 2 * HD + EXTRA
    small_acc[vec_at + 4 : vec_at + 5] = jnp.sum(
        slope_one * first + slope_two * next_one, axis=0, keepdims=True
    )
    carry[...] = jnp.zeros_like(carry)

    def weight_grad_copy(index, peer, slot):
        src = (hid, gprime)[index].at[pl.ds(pl.multiple_of(peer * shard, shard), shard)]
        dst = (ug_recv, dg_recv)[index].at[pl.ds(pl.multiple_of(slot * shard, shard), shard)]
        return to_dp(src, dst, g_send.at[index, peer], g_recv.at[index, slot], peer)

    def backward(step, none):
        loop = LOOPS - 1 - step
        info = meta_ref[loop, own_rows]
        running = info[:, RUN_LANE : RUN_LANE + 1]
        after = sgrad[loop] + carry[...]
        branch = after * running
        rows_all[me] = branch.astype(BF16)
        gather_start(rows_all, ag_send, ag_recv, n_act)
        gather_finish(rows_all, ag_send, ag_recv, n_act)
        places = gather_matrix(loop)
        grad_rows = nn(places, rows_all[0:n_act].reshape(valid_rows, width))
        gate = fgate_k[cap_rows(loop)]
        gate_grad = jnp.sum(grad_rows * part_k[cap_rows(loop)], axis=1, keepdims=True)
        scaled = (grad_rows * gate).astype(BF16)
        rows_in = rows_k[cap_rows(loop)]
        part_k[cap_rows(loop)] = jnp.zeros((cap, width), F32)

        def hidden_tile(tile, none):
            cols = pl.ds(pl.multiple_of(tile * TILE, TILE), TILE)
            hidden = hid[cap_rows(loop), cols]
            down_acc[:, cols] += tn(scaled, hidden)
            inner_grad = (
                nn(scaled, down_w[:, cols]) * gprime[cap_rows(loop), cols].astype(F32)
            ).astype(BF16)
            up_acc[:, cols] += tn(rows_in, inner_grad)
            part_k[cap_rows(loop)] += nt(inner_grad, up_w[:, cols])
            return none

        lax.fori_loop(0, up_w.shape[1] // TILE, hidden_tile, 0)
        terms = part_k[cap_rows(loop)].astype(BF16)
        high = gate_grad.astype(BF16).astype(F32)
        spread = jnp.where(lane_cap == n_exp + me, high, 0.0) + jnp.where(
            lane_cap == me, gate_grad - high, 0.0
        )
        spread_t = jnp.transpose(spread)[0:EXTRA].astype(BF16)

        def row_terms(block):
            matrix = scatter_matrix(loop, block)
            grads = nt(spread_t, matrix)
            return jnp.concatenate(
                [
                    nn(matrix, terms),
                    jnp.concatenate([grads, jnp.zeros((EXTRA, width - own), F32)], axis=1),
                ],
                axis=0,
            )

        reduce_blocks(
            row_terms,
            n_act,
            own + EXTRA,
            pair_send,
            pair_recv,
            far_send,
            far_recv,
            rs_sems,
            total,
        )

        @pl.when(loop == 0)
        def _():
            hid[0:width] = up_acc[...].astype(BF16)
            each_peer(lambda peer: weight_grad_copy(0, peer, dp).start())
            gprime[0:width] = down_acc[...].astype(BF16)
            each_peer(lambda peer: weight_grad_copy(1, peer, dp).start())

        second_grad = total[0:own]
        gate_rows = total[own : own + n_exp, 0:own] + total[own + n_exp : own + 2 * n_exp, 0:own]
        gate_rows = jnp.concatenate(
            [jnp.zeros((n_exp, own), F32), gate_rows, jnp.zeros((LANES - 2 * n_exp, own), F32)],
            axis=0,
        )
        gate_grads = jnp.transpose(gate_rows)
        second = second_k[loop]
        gates = masked_softmax(
            nn(second, rb[...]), (info > 0.5) & (lane >= n_exp) & (lane < 2 * n_exp)
        )
        logit_grad = (
            gates * (gate_grads - jnp.sum(gates * gate_grads, axis=1, keepdims=True))
        ).astype(BF16)
        small_acc[2 * HD : vec_at] += tn(logit_grad, second)[0:EXTRA]
        second_grad = second_grad + nt(logit_grad, rb[...])
        unit, inverse = normalise(middle[loop])
        small_acc[vec_at + 2 : vec_at + 3] += jnp.sum(second_grad * unit, axis=0, keepdims=True)
        small_acc[vec_at + 3 : vec_at + 4] += jnp.sum(second_grad, axis=0, keepdims=True)
        middle_grad = norm_back(second_grad, unit, inverse, gain_two) + branch

        normed = normed_k[loop]
        gates = gate_k[loop]
        kv_rows = window_keys(loop)
        mix[...] = jnp.zeros_like(mix)
        dga[...] = jnp.zeros_like(dga)
        dkv_t[...] = jnp.zeros_like(dkv_t)

        def attend_back(pair, none):
            rows = pl.ds(pl.multiple_of(pair * 2 * own, 2 * own), 2 * own)
            outs = o_k[loop, rows]
            out_grads, parts = [], []
            for half in range(2):
                expert = 2 * pair + half
                out_half = outs[half * own : (half + 1) * own]
                gate = column(gates, expert, lane)
                dot = jnp.sum(middle_grad * nt(out_half, w_all[expert]), axis=1, keepdims=True)
                dga[...] += jnp.where(lane == expert, dot, 0.0)
                part_grad = (gate * middle_grad).astype(BF16)
                parts.append(part_grad)
                out_grads.append(
                    jnp.where(lane < HD, 0.0, nn(part_grad, w_all[expert])).astype(BF16)
                )
            out_grad = jnp.concatenate(out_grads, axis=0)
            prob_low = p_k[loop, rows]
            prob = prob_low.astype(F32)
            prob_grad = nt(out_grad, kv_rows)
            centre = jnp.sum(prob * prob_grad, axis=1, keepdims=True)
            score_grad = (prob * (prob_grad - centre)).astype(BF16)
            query_grad = jnp.where(lane_two < HD, nn(score_grad, kv_rows) * scale, 0.0).astype(BF16)
            query = q_k[loop, rows]
            dkv_t[...] += tn(query, score_grad) * scale + tn(out_grad, prob_low)
            for half in range(2):
                expert = 2 * pair + half
                cut = slice(half * own, (half + 1) * own)
                attn_acc[expert] += tn(query_grad[cut], normed) + tn(outs[cut], parts[half])
                mix[...] += nt(query_grad[cut], w_all[expert])
            return none

        lax.fori_loop(0, n_exp // 2, attend_back, 0)
        for block in range(window):
            grads = jnp.transpose(dkv_t[:, block * own : (block + 1) * own])
            dkv[block] = grads
            dkv_send[block] = grads.astype(BF16)

        def kv_copy(distance, owner):
            return to_expert(
                dkv_send.at[jnp.clip(owner - win_at, 0, window - 1)],
                dkv_recv.at[distance - 1],
                dk_send.at[distance - 1],
                dk_recv.at[distance - 1],
                owner,
            )

        for distance in range(1, window):

            @pl.when(active & (me >= distance))
            def _():
                kv_copy(distance, me - distance).start()

        gate_grads = dga[...]
        logit_grad = (
            gates * (gate_grads - jnp.sum(gates * gate_grads, axis=1, keepdims=True))
        ).astype(BF16)
        small_acc[2 * HD : vec_at] += tn(logit_grad, normed)[0:EXTRA]
        normed_grad = mix[...] + nt(logit_grad, rb[...])
        unit, inverse = normalise(state[loop])

        own_block = jnp.clip(me - win_at, 0, window - 1)
        dkv[window] = jnp.where(active, dkv[own_block], 0.0)
        for distance in range(1, window):

            @pl.when(me + distance < n_act)
            def _():
                to_expert(
                    dkv_send.at[0],
                    dkv_recv.at[distance - 1],
                    dk_send.at[distance - 1],
                    dk_recv.at[distance - 1],
                    me + distance,
                ).wait_recv()
                dkv[window] += dkv_recv[distance - 1].astype(F32)

        for distance in range(1, window):

            @pl.when(active & (me >= distance))
            def _():
                kv_copy(distance, me - distance).wait_send()

        kv_grad = dkv[window].astype(BF16)
        small_acc[0 : 2 * HD] += tn(kv_grad, normed)
        normed_grad = normed_grad + nt(kv_grad, kvb[...])
        small_acc[vec_at : vec_at + 1] += jnp.sum(normed_grad * unit, axis=0, keepdims=True)
        small_acc[vec_at + 1 : vec_at + 2] += jnp.sum(normed_grad, axis=0, keepdims=True)
        carry[...] = (
            after * (1.0 - running)
            + middle_grad
            + norm_back(normed_grad, unit, inverse, gain_one)
        )
        return none

    lax.fori_loop(0, LOOPS, backward, 0)
    xgrad_ref[...] = carry[...]

    chunk = small_acc.shape[0] // n_exp
    reduce_blocks(
        lambda block: small_acc[pl.ds(pl.multiple_of(block * chunk, chunk), chunk)],
        n_exp,
        chunk,
        s_pair_send,
        s_pair_recv,
        s_far_send,
        s_far_recv,
        s_sems,
        s_total,
    )
    s_dp[dp] = s_total[...].astype(BF16)

    def small_copy(peer, slot):
        return to_dp(s_dp.at[slot], s_dp.at[slot], t_send.at[0, peer], t_recv.at[0, slot], peer)

    each_peer(lambda peer: small_copy(peer, dp).start())

    reduce_blocks(
        lambda block: jnp.transpose(attn_acc[block]),
        n_exp,
        width,
        a_pair_send,
        a_pair_recv,
        a_far_send,
        a_far_recv,
        a_sems,
        a_total,
    )
    a_stage[...] = a_total[...].astype(BF16)

    def attn_copy(peer, slot):
        src = a_stage.at[pl.ds(pl.multiple_of(peer * shard, shard), shard)]
        dst = a_recv.at[pl.ds(pl.multiple_of(slot * shard, shard), shard)]
        return to_dp(src, dst, t_send.at[1, peer], t_recv.at[1, slot], peer)

    each_peer(lambda peer: attn_copy(peer, dp).start())

    each_peer(lambda peer: small_copy(peer, peer).wait_recv())
    s_total[...] = jnp.zeros_like(s_total)

    def add_small(index, none):
        s_total[...] += s_dp[index].astype(F32)
        return none

    lax.fori_loop(0, n_dp, add_small, 0)
    s_all[me] = s_total[...]
    gather_start(s_all, sg_send, sg_recv, n_exp)

    each_peer(lambda peer: attn_copy(peer, peer).wait_recv())
    agrad_ref[...] = a_total[dp_rows]

    def add_attn(peer):
        rows = pl.ds(pl.multiple_of(peer * shard, shard), shard)
        agrad_ref[...] += a_recv[rows].astype(F32)

    each_peer(add_attn)
    ugrad_ref[...] = up_acc[dp_rows]
    dgrad_ref[...] = down_acc[dp_rows]

    def add_up(peer):
        rows = pl.ds(pl.multiple_of(peer * shard, shard), shard)
        weight_grad_copy(0, peer, peer).wait_recv()
        ugrad_ref[...] += ug_recv[rows].astype(F32)

    def add_down(peer):
        rows = pl.ds(pl.multiple_of(peer * shard, shard), shard)
        weight_grad_copy(1, peer, peer).wait_recv()
        dgrad_ref[...] += dg_recv[rows].astype(F32)

    each_peer(add_up)
    each_peer(add_down)
    gather_finish(s_all, sg_send, sg_recv, n_exp)
    small_ref[...] = s_all[...]

    def sent(peer):
        for index in range(3):
            weight_copy(index, peer, dp).wait_send()
        for index in range(2):
            weight_grad_copy(index, peer, dp).wait_send()
        small_copy(peer, dp).wait_send()
        attn_copy(peer, dp).wait_send()

    each_peer(sent)


def per_device(
    block_input,
    cotangent,
    lengths,
    run_loops,
    attn_routes,
    ffn_routes,
    shared_vectors,
    shared_moment,
    shared_second,
    key_value,
    kv_moment,
    kv_second,
    router_weights,
    router_moment,
    router_second,
    attn_weights,
    attn_moment,
    attn_second,
    up_weights,
    up_moment,
    up_second,
    down_weights,
    down_moment,
    down_second,
):
    n_exp = lax.axis_size("expert")
    n_dp = lax.axis_size("dp")
    me = lax.axis_index("expert")
    own, width = block_input.shape
    row_total = run_loops.shape[0]
    shard = attn_weights.shape[1]
    hidden = up_weights.shape[2]
    cap = 5 * row_total * KFF // (4 * n_exp)
    n_act = FILLED // own
    window = min(n_act, MAXLEN // own + 1)
    pairs = n_exp // 2
    valid_rows = n_act * own

    positions = jnp.arange(row_total, dtype=jnp.int32)
    bounds = jnp.cumsum(lengths[0])
    segment = jnp.sum((positions[:, None] >= bounds[None, :]).astype(jnp.int32), axis=1)
    valid = segment < lengths.shape[1]
    loops = jnp.arange(LOOPS, dtype=jnp.int32)
    running = valid[None, :] & (loops[:, None] < run_loops[None, :])
    selected = jnp.any(ffn_routes == me, axis=2) & running
    ranks = jnp.where(selected, jnp.cumsum(selected.astype(jnp.int32), axis=1) - 1, -1).astype(F32)
    lane = jnp.arange(LANES, dtype=jnp.int32)
    chosen = jnp.any(attn_routes[..., None] == lane, axis=2) | jnp.any(
        ffn_routes[..., None] + n_exp == lane, axis=2
    )
    seg_rows = segment.astype(F32)
    meta = jnp.where(
        lane == RANK_LANE,
        ranks[..., None],
        jnp.where(
            lane == RUN_LANE,
            running.astype(F32)[..., None],
            jnp.where(lane == SEG_LANE, seg_rows[None, :, None], chosen.astype(F32)),
        ),
    )
    row_meta = jnp.concatenate([ranks, seg_rows[None]], axis=0)[:, None, :]
    vectors = jnp.pad(shared_vectors, ((0, 3), (0, 0)))
    router = jnp.pad(router_weights, ((0, 0), (0, LANES - router_weights.shape[1])))

    small_rows = 32 * n_exp
    vmem = pltpu.VMEM
    dma = pltpu.SemaphoreType.DMA
    block = (pairs, own + EXTRA, width)
    attn_block = (pairs, width, 2 * HD)
    small_block = (pairs, 32, width)
    scratch = [
        vmem((width, 2 * HD), BF16),
        vmem((width, LANES), BF16),
        vmem((n_exp, width, 2 * HD), BF16),
        vmem((width, hidden), BF16),
        vmem((width, hidden), BF16),
        vmem((width, hidden), F32),
        vmem((width, hidden), F32),
        vmem((n_exp, 2 * HD, width), F32),
        vmem((small_rows, width), F32),
        vmem((LOOPS + 1, own, width), F32),
        vmem((LOOPS, own, width), F32),
        vmem((LOOPS, own, width), BF16),
        vmem((LOOPS, own, width), BF16),
        vmem((LOOPS, n_exp, own, 2 * HD), BF16),
        vmem((LOOPS, n_exp * own, 2 * HD), BF16),
        vmem((LOOPS, n_exp * own, 2 * HD), BF16),
        vmem((LOOPS, n_exp * own, window * own), BF16),
        vmem((own, window * own), F32),
        vmem((own, width), F32),
        vmem((own, LANES), F32),
        vmem((2 * HD, window * own), F32),
        vmem((window + 1, own, 2 * HD), F32),
        vmem((LOOPS, own, LANES), F32),
        vmem((n_exp, own, width), BF16),
        vmem((LOOPS * cap, width), BF16),
        vmem((LOOPS * cap, hidden), BF16),
        vmem((LOOPS * cap, hidden), BF16),
        vmem((LOOPS * cap, width), F32),
        vmem((LOOPS * cap, 1), F32),
        vmem((LOOPS, own, width), F32),
        vmem((own, width), F32),
        vmem((own + EXTRA, width), F32),
        vmem(block, BF16),
        vmem(block, BF16),
        vmem(block, BF16),
        vmem(block, BF16),
        vmem((window, own, 2 * HD), BF16),
        vmem((window, own, 2 * HD), BF16),
        vmem((width, hidden), BF16),
        vmem((width, hidden), BF16),
        vmem(attn_block, BF16),
        vmem(attn_block, BF16),
        vmem(attn_block, BF16),
        vmem(attn_block, BF16),
        vmem((width, 2 * HD), F32),
        vmem((width, 2 * HD), BF16),
        vmem((width, 2 * HD), BF16),
        vmem(small_block, BF16),
        vmem(small_block, BF16),
        vmem(small_block, BF16),
        vmem(small_block, BF16),
        vmem((32, width), F32),
        vmem((n_dp, 32, width), BF16),
        vmem((n_exp, 32, width), F32),
        dma((3, n_dp)),
        dma((3, n_dp)),
        dma((2 * pairs,)),
        dma((n_exp,)),
        dma((2 * pairs,)),
        dma((n_exp,)),
        dma((2 * pairs,)),
        dma((n_exp,)),
        dma((2 * pairs,)),
        dma((n_exp,)),
        dma((4, pairs)),
        dma((4, pairs)),
        dma((4, pairs)),
        dma((window,)),
        dma((window,)),
        dma((2, n_dp)),
        dma((2, n_dp)),
        dma((2, n_dp)),
        dma((2, n_dp)),
    ]
    whole = pl.BlockSpec(memory_space=pltpu.VMEM)
    output, input_grad, up_sum, down_sum, attn_sum, small = pl.pallas_call(
        functools.partial(block_kernel, n_exp, n_dp, n_act, cap),
        out_shape=(
            jax.ShapeDtypeStruct((own, width), F32),
            jax.ShapeDtypeStruct((own, width), F32),
            jax.ShapeDtypeStruct((shard, hidden), F32),
            jax.ShapeDtypeStruct((shard, hidden), F32),
            jax.ShapeDtypeStruct((shard, 2 * HD), F32),
            jax.ShapeDtypeStruct((n_exp, 32, width), F32),
        ),
        in_specs=[whole] * 10,
        out_specs=[whole] * 6,
        scratch_shapes=scratch,
        compiler_params=pltpu.CompilerParams(
            collective_id=0, has_side_effects=True, vmem_limit_bytes=62 * 1024 * 1024
        ),
        name="block",
    )(
        block_input,
        cotangent,
        meta,
        row_meta,
        vectors,
        key_value,
        router,
        attn_weights[0],
        up_weights[0],
        down_weights[0],
    )

    small = small.reshape(small_rows, width)
    kv_sum = small[: 2 * HD].T
    router_sum = small[2 * HD : 2 * HD + 2 * n_exp].T
    shared_sum = small[2 * HD + EXTRA : 2 * HD + EXTRA + 5]
    shared_rates = jnp.array([6.0, 6.0, 6.0, 6.0, 20.0 / math.sqrt(D)], dtype=F32)[:, None]
    attn_rates = jnp.concatenate(
        [
            jnp.full((HD,), 25.0 / math.sqrt(D), F32),
            jnp.full((HD,), 50.0 / math.sqrt(HD), F32),
        ]
    )
    shared_new = adam_update(
        shared_vectors, shared_moment, shared_second, shared_sum, shared_rates, 0.0
    )
    kv_new = adam_update(key_value, kv_moment, kv_second, kv_sum, 20.0 / math.sqrt(D), decay_rate)
    router_new = adam_update(
        router_weights,
        router_moment,
        router_second,
        router_sum,
        50.0 / math.sqrt(3 * D),
        decay_rate,
    )
    attn_new = adam_update(
        attn_weights, attn_moment, attn_second, attn_sum[None], attn_rates, decay_rate
    )
    up_new = adam_update(
        up_weights, up_moment, up_second, up_sum[None], 14.0 / math.sqrt(D), decay_rate
    )
    down_new = adam_update(
        down_weights, down_moment, down_second, down_sum[None], 17.0 / math.sqrt(FF), decay_rate
    )
    return (
        output,
        input_grad,
        *shared_new,
        *kv_new,
        *router_new,
        *attn_new,
        attn_new[0].astype(BF16),
        *up_new,
        up_new[0].astype(BF16),
        *down_new,
        down_new[0].astype(BF16),
    )


def solution(mesh):
    rows = P(("dp", "expert"), None)
    weights = P("expert", "dp", None)
    return jax.shard_map(
        per_device,
        mesh=mesh,
        in_specs=(
            rows,
            rows,
            P("dp", None),
            P("dp"),
            P(None, "dp", None),
            P(None, "dp", None),
            *([P()] * 9),
            *([weights] * 9),
        ),
        out_specs=(rows, rows, *([P()] * 9), *([weights] * 12)),
        check_vma=False,
    )
```

time: 1750 us -> 367 us (0.21)
  waiting for transfers between devices: 978 us -> 0 us
  Pallas kernels: 0 us -> 337 us
  other arithmetic: 305 us -> 25.2 us
  local copies, waits for them, and re-layouts: 274 us -> 3.95 us
  matrix products: 112 us -> 0 us
  blocking collectives: 48.9 us -> 0 us
  between operations: 20.4 us -> 0.96 us
    reduce_scatter x24 -> x0, waiting for transfers between devices: 574 us -> none  [the longest x3 108 us: per_device(): lax.psum_scatter(attn_in_part, 'expert', scatter_dimension=0, tiled=True)]
    pallas_call x0 -> x1, Pallas kernels: none -> 337 us  [per_device(): pl.pallas_call(functools.partial(block_kernel, n_exp, n_dp, n_act, cap),...]
    all_gather x14 -> x0, waiting for transfers between devices: 276 us -> none  [the longest x3 83.9 us: per_device(): attn_grad_all = lax.all_gather(middle_grad, 'expert', axis=0, tiled=True)]
    scatter-add x34 -> x0, other arithmetic: 213 us -> none  [the longest x16 104 us: dense_gates(): picked = jnp.take_along_axis(logits, chosen, axis=1)]
    gather x84 -> x0, local copies, waits for them, and re-layouts: 209 us -> none  [the longest x60 133 us: dense_gates(): picked = jnp.take_along_axis(logits, chosen, axis=1)]
    psum x1 -> x0, waiting for transfers between devices: 127 us -> none  [per_device(): lax.psum((shared_part, kv_acc, router_part), ('dp', 'expert'))]
    dot_general x87 -> x0, matrix products: 112 us -> none  [the longest x54 70.1 us: contract(): lax.dot_general(left, right, (((left_dim,), (right_dim,)), ((), ())), pre...]
    psum x1 -> x0, blocking collectives: 38.3 us -> none  [per_device(): lax.psum((shared_part, kv_acc, router_part), ('dp', 'expert'))]
  transfers between devices with their start and end apart: 39 -> 0, of which waited for: 37 -> 0; matrix products, arithmetic and copies ran while one was open for 20% -> 0% of each run, Pallas kernels for 0% -> 0%
where the time goes in v1:
time: 367 us
  Pallas kernels  337 us (92%)
  other arithmetic  25.2 us (7%)
  local copies, waits for them, and re-layouts  3.95 us (1%)
    pallas_call x1, Pallas kernels, per_device(): pl.pallas_call(functools.partial(block_kernel, n_exp, n_dp, n_act, cap),...  337 us

profile of v1, /device:TPU:0, one launch (start us, length us, event | category | flops | bytes accessed | tf_op | source)
XLA Modules:
  0.0 366.6 jit_solution(10631471182252545288)
XLA Ops:
  0.7 0.8 reduce-window.18
  1.5 0.1 convert_reduce_fusion
  1.6 0.8 compare_reduce_fusion
  2.4 0.7 fusion.16
  3.1 0.8 reduce-window.19
  3.9 0.2 slice_reduce_fusion
  4.1 0.2 reduce-window.20
  4.3 0.1 add_bitcast_fusion
  4.4 0.7 fusion.12
  5.1 0.7 fusion.17
  5.8 0.8 broadcast_add_fusion
  6.6 0.0 copy-start.12
  6.6 1.3 fusion.1
  8.0 4.4 %fusion = pred[3,1024,128]{2,1,0:T(8,128)(4,1)S(1)} fusion(s32[3,1024,4]{1,2,0:T(4,128)} %param.29), kind=kLoop, calls=%fused_computation.1 | loop fusion | flops 2752512 | bytes 442368 | tf_op jit(solution)/shard_map/reduce_or | solution.py:855
  12.4 0.0 copy-start.16
  12.4 2.4 select_select_fusion.meta_ref
  14.8 0.6 broadcast_in_dim.60.rowm_ref
  15.4 0.0 copy-done.12
  15.4 0.1 copy.56
  15.5 0.7 pad.9.rw_ref
  16.3 0.0 copy-done.16
  16.3 0.6 pad.8.vec_ref
  16.9 0.0 copy-start.17
  16.9 0.0 copy-start.22
  16.9 0.0 copy-start
  16.9 336.6 %block.1 = (f32[128,512]{1,0:T(8,128)}, f32[128,512]{1,0:T(8,128)}, f32[128,2048]{1,0:T(8,128)}, f32[128,2048]{1,0:T(8,128)}, f32[128,128]{1,0:T(8,128)}, /*index=5*/f32[8,32,512]{2,1,0:T(8,128)}) custom-call(bf16[128,512]{1,0:T(8,128)(2,1)} %x_ref.1, bf16[128,512]{1,0:T(8,128)(2,1)} %cot_ref.1, f32[3,1024,128]{2,1,0:T(8,128)} %select_select_fusion.meta_ref, ...), custom_call_target="tpu_custom_call" | custom-call | tf_op jit(solution)/shard_map/block/pallas_call | solution.py:954
  353.5 0.0 copy-done.17
  353.5 0.0 copy-done.18
  353.5 1.4 multiply_subtract_fusion.4
  354.9 0.0 copy-done.19
  354.9 0.0 copy-done.20
  354.9 0.0 copy-done.22
  354.9 1.4 multiply_subtract_fusion.5
  356.3 0.0 copy-done
  356.3 0.0 copy-start.4
  356.3 4.4 %fusion.20 = (bf16[1,128,2048]{2,1,0:T(8,128)(2,1)}, f32[1,128,2048]{2,1,0:T(8,128)}, f32[1,128,2048]{2,1,0:T(8,128)}, f32[1,128,2048]{2,1,0:T(8,128)}) fusion(f32[1,128,2048]{2,1,0:T(8,128)S(1)} %copy-done, f32[128,2048]{1,0:T(8,128)} %get-tuple-element.33, f32[1,128,2048]{2,1,0:T(8,128)} %param.44, f32[1,128,2048]{2,1,0:T(8,128)} %param.45), kind=kLoop, calls=%fused_computation.55 | loop fusion | flops 4194304 | bytes 7864320 | tf_op jit(solution)/shard_map/convert_element_type | solution.py:1025
  360.8 0.0 copy-done.1
  360.8 0.0 copy-done.2
  360.8 0.0 copy-done.3
  360.8 0.0 copy-done.4
  360.8 0.0 copy-start.11
  360.8 0.0 copy-start.5
  360.8 0.0 copy-start.7
  360.8 0.0 copy-start.8
  360.9 2.4 fusion.18
  363.3 0.0 copy-start.21
  363.3 0.0 copy-done.11
  363.3 0.0 copy-start.10
  363.3 0.0 copy-start.9
  363.3 0.1 copy.57
  363.5 0.0 copy-done.5
  363.5 0.0 copy-done.7
  363.5 0.0 copy-done.8
  363.5 1.0 multiply_subtract_fusion.2
  364.5 0.0 copy-done.6
  364.5 0.0 copy-done.13
  364.5 0.0 copy-done.14
  364.5 0.0 copy-done.15
  364.5 0.0 copy-done.21
  364.5 0.7 fusion.22
  365.2 0.0 copy-done.10
  365.2 0.7 copy.64
  365.9 0.0 copy-done.9
  365.9 0.7 copy.65
  (17 shorter events, 0.1 us)
Async XLA Ops:
  6.6 8.8 %copy-start.12 = (f32[512,16]{0,1:T(8,128)S(1)}, f32[512,16]{0,1:T(8,128)}, u32[]{:S(2)}) copy-start(f32[512,16]{0,1:T(8,128)} %param.37) | copy-start | bytes 98308
  12.4 3.9 %copy-start.16 = (f32[5,512]{1,0:T(8,128)S(1)}, f32[5,512]{1,0:T(8,128)}, u32[]{:S(2)}) copy-start(f32[5,512]{1,0:T(8,128)} %param.31) | copy-start | bytes 30724
  16.9 336.6 %copy-start.17 = (f32[512,16]{0,1:T(8,128)S(1)}, f32[512,16]{0,1:T(8,128)}, u32[]{:S(2)}) copy-start(f32[512,16]{0,1:T(8,128)} %param.38) | copy-start | bytes 98308
  16.9 336.6 %copy-start.18 = (f32[512,16]{0,1:T(8,128)S(1)}, f32[512,16]{0,1:T(8,128)}, u32[]{:S(2)}) copy-start(f32[512,16]{0,1:T(8,128)} %param.39) | copy-start | bytes 98308
  16.9 338.0 %copy-start.19 = (f32[5,512]{1,0:T(8,128)S(1)}, f32[5,512]{1,0:T(8,128)}, u32[]{:S(2)}) copy-start(f32[5,512]{1,0:T(8,128)} %param.32) | copy-start | bytes 30724
  16.9 338.0 %copy-start.20 = (f32[5,512]{1,0:T(8,128)S(1)}, f32[5,512]{1,0:T(8,128)}, u32[]{:S(2)}) copy-start(f32[5,512]{1,0:T(8,128)} %param.33) | copy-start | bytes 30724
  16.9 338.0 %copy-start.22 = (f32[5]{0:T(128)S(1)}, f32[5]{0:T(128)}, u32[]{:S(2)}) copy-start(f32[5]{0:T(128)} %constant.47.clone) | copy-start | bytes 64
  16.9 339.4 %copy-start = (f32[1,128,2048]{2,1,0:T(8,128)S(1)}, f32[1,128,2048]{2,1,0:T(8,128)}, u32[]{:S(2)}) copy-start(f32[1,128,2048]{2,1,0:T(8,128)} %param.43) | copy-start | bytes 3145732
  356.3 4.5 %copy-start.1 = (f32[1,128,2048]{2,1,0:T(8,128)S(1)}, f32[1,128,2048]{2,1,0:T(8,128)}, u32[]{:S(2)}) copy-start(f32[1,128,2048]{2,1,0:T(8,128)} %param.46) | copy-start | bytes 3145732
  356.3 4.5 %copy-start.2 = (f32[1,128,2048]{2,1,0:T(8,128)S(1)}, f32[1,128,2048]{2,1,0:T(8,128)}, u32[]{:S(2)}) copy-start(f32[1,128,2048]{2,1,0:T(8,128)} %param.47) | copy-start | bytes 3145732
  356.3 4.5 %copy-start.3 = (f32[1,128,2048]{2,1,0:T(8,128)S(1)}, f32[1,128,2048]{2,1,0:T(8,128)}, u32[]{:S(2)}) copy-start(f32[1,128,2048]{2,1,0:T(8,128)} %param.48) | copy-start | bytes 3145732
  356.3 4.5 %copy-start.4 = (f32[128,2048]{1,0:T(8,128)S(1)}, f32[128,2048]{1,0:T(8,128)}, u32[]{:S(2)}) copy-start(f32[128,2048]{1,0:T(8,128)} %get-tuple-element.34) | copy-start | bytes 3145732
  360.8 2.5 copy-start.11
  360.8 2.7 copy-start.5
  360.8 2.7 copy-start.7
  360.8 2.6 copy-start.8
  363.3 1.2 copy-start.6
  363.3 1.2 copy-start.13
  363.3 1.2 copy-start.14
  363.3 1.2 copy-start.15
  363.3 1.2 copy-start.21
  363.3 1.9 copy-start.10
  363.3 2.6 copy-start.9

commit v2 on v1

v2 whole, which is shorter than its diff:
```python
import functools
import math

import jax
import jax.numpy as jnp
from jax import lax
from jax.experimental import pallas as pl
from jax.experimental.pallas import tpu as pltpu
from jax.sharding import PartitionSpec as P

D = 512
HD = 64
FF = 2048
KATT = 4
KFF = 2
LOOPS = 3
STEP = 10
MAXLEN = 512
FILLED = 896

ln_eps = 1e-05
beta_one = 0.9
beta_two = 0.999
adam_eps = 1e-08
decay_rate = 0.01
masked_score = -1e30

F32 = jnp.float32
BF16 = jnp.bfloat16
MESH = pl.DeviceIdType.MESH
LANES = 128
RANK_LANE = 16
RUN_LANE = 17
SEG_LANE = 18
INFO = 32
TILE = 512
EXTRA = 16


def nn(left, right):
    return lax.dot_general(left, right, (((1,), (0,)), ((), ())), preferred_element_type=F32)


def nt(left, right):
    return lax.dot_general(left, right, (((1,), (1,)), ((), ())), preferred_element_type=F32)


def tn(left, right):
    return lax.dot_general(left, right, (((0,), (0,)), ((), ())), preferred_element_type=F32)


def normalise(values):
    centre = values - jnp.mean(values, axis=-1, keepdims=True)
    inverse = lax.rsqrt(jnp.mean(centre * centre, axis=-1, keepdims=True) + ln_eps)
    return centre * inverse, inverse


def norm_back(grad, unit, inverse, gain):
    scaled = grad * gain
    first = jnp.mean(scaled, axis=-1, keepdims=True)
    second = jnp.mean(scaled * unit, axis=-1, keepdims=True)
    return inverse * (scaled - first - unit * second)


def masked_softmax(logits, valid):
    top = jnp.max(jnp.where(valid, logits, masked_score), axis=-1, keepdims=True)
    powers = jnp.where(valid, jnp.exp(jnp.where(valid, logits - top, 0.0)), 0.0)
    return powers / jnp.maximum(jnp.sum(powers, axis=-1, keepdims=True), 0.5)


def adam_update(weight, moment, second, grad, rate, decay):
    moment_new = beta_one * moment + (1.0 - beta_one) * grad
    second_new = beta_two * second + (1.0 - beta_two) * grad * grad
    moment_hat = moment_new * (1.0 / (1.0 - beta_one**STEP))
    second_hat = second_new * (1.0 / (1.0 - beta_two**STEP))
    weight_new = weight - rate * (moment_hat / (jnp.sqrt(second_hat) + adam_eps) + decay * weight)
    return (weight_new, moment_new, second_new)


def block_kernel(
    n_exp,
    n_dp,
    n_act,
    cap,
    x_ref,
    cot_ref,
    len_ref,
    run_ref,
    ar_ref,
    fr_ref,
    vec_ref,
    kvw_ref,
    rw_ref,
    aw_ref,
    uw_hbm,
    dw_hbm,
    out_ref,
    xgrad_ref,
    ugrad_ref,
    dgrad_ref,
    agrad_ref,
    kvgrad_ref,
    rgrad_ref,
    vgrad_ref,
    meta_ref,
    rowm_ref,
    kvb,
    rb,
    w_all,
    up_w,
    down_w,
    up_acc,
    down_acc,
    attn_acc,
    small_acc,
    state,
    middle,
    normed_k,
    second_k,
    kv_k,
    q_k,
    o_k,
    p_k,
    ds_k,
    bias,
    mix,
    dga,
    dkv_t,
    dkv,
    gate_k,
    rows_all,
    rows_two,
    gather_m,
    scatter_m,
    rows_k,
    hid,
    gprime,
    row_grads,
    part_k,
    fgate_k,
    ggrad,
    scaled_k,
    sgrad,
    carry,
    mgrad,
    total,
    total_two,
    pair_send,
    pair_recv,
    far_send,
    far_recv,
    pair_send_two,
    pair_recv_two,
    far_send_two,
    far_recv_two,
    dkv_send,
    dkv_recv,
    u_first,
    u_last,
    d_first,
    d_last,
    a_total,
    a_stage,
    a_recv,
    s_pair_send,
    s_pair_recv,
    s_far_send,
    s_far_recv,
    s_total,
    s_dp,
    s_all,
    in_sems,
    w_send,
    w_recv,
    uw_send,
    uw_recv,
    uw_send_two,
    uw_recv_two,
    dw_send,
    dw_recv,
    dw_send_two,
    dw_recv_two,
    ag_send,
    ag_recv,
    bg_send,
    bg_recv,
    wg_send,
    wg_recv,
    sg_send,
    sg_recv,
    kg_send,
    kg_recv,
    rs_sems,
    rs_sems_two,
    s_sems,
    a_sems,
    dk_send,
    dk_recv,
    ug_send,
    ug_recv,
    ug_send_two,
    ug_recv_two,
    dg_send,
    dg_recv,
    dg_send_two,
    dg_recv_two,
    t_send,
    t_recv,
):
    me = lax.axis_index("expert")
    dp = lax.axis_index("dp")
    pairs = n_exp // 2
    core = lax.rem(me, 2)
    chip = lax.div(me, 2)
    sibling = 2 * chip + 1 - core
    n_low, n_high = dp_grid(n_dp)
    high = lax.div(dp, n_low)
    low = lax.rem(dp, n_low)
    own = x_ref.shape[0]
    width = x_ref.shape[1]
    slots = run_ref.shape[1]
    shard = aw_ref.shape[0]
    hidden_units = up_w.shape[1]
    tiles = hidden_units // TILE
    valid_rows = n_act * own
    window = min(n_act, MAXLEN // own + 1)
    keys = window * own
    win_at = jnp.clip(me - (window - 1), 0, n_act - window)
    scale = HD ** (-0.5)
    active = me < n_act
    last = LOOPS - 1

    def remote(src, dst, send, recv, **where):
        return pltpu.make_async_remote_copy(
            src_ref=src,
            dst_ref=dst,
            send_sem=send,
            recv_sem=recv,
            device_id=where,
            device_id_type=MESH,
        )

    def shard_rows(index, count=1):
        return pl.ds(pl.multiple_of(index * shard, shard), count * shard)

    def each_peer(body):
        def step(k, none):
            body(lax.rem(dp + k, n_dp))
            return none

        lax.fori_loop(1, n_dp, step, 0)

    def high_peers():
        return [lax.rem(high + k, n_high) for k in range(1, n_high)]

    def low_peers():
        return [lax.rem(low + k, n_low) for k in range(1, n_low)]

    class Gather:
        def __init__(self, buf, send, recv, count):
            self.buf, self.send, self.recv, self.count = buf, send, recv, count

        def copy(self, block, sem, where):
            ref = self.buf.at[block]
            return remote(ref, ref, self.send.at[sem], self.recv.at[block], expert=where)

        def start(self):
            @pl.when(me < self.count)
            def _():
                for k in range(1, pairs):
                    zz = lax.rem(chip + k, pairs)
                    self.copy(me, zz, 2 * zz + core).start()
                self.copy(me, chip, sibling).start()

        def finish(self):
            for k in range(pairs - 1, 0, -1):
                zz = lax.rem(chip + k, pairs)
                src = 2 * zz + core

                @pl.when(src < self.count)
                def _():
                    self.copy(src, zz, src).wait_recv()
                    self.copy(src, pairs + zz, sibling).start()

            for k in range(pairs):
                zz = lax.rem(chip + k, pairs)
                src = 2 * zz + 1 - core

                @pl.when(src < self.count)
                def _():
                    self.copy(src, zz, sibling).wait_recv()

            @pl.when(me < self.count)
            def _():
                for k in range(1, pairs):
                    zz = lax.rem(chip + k, pairs)
                    self.copy(me, zz, 2 * zz + core).wait_send()
                self.copy(me, chip, sibling).wait_send()

            for k in range(1, pairs):
                zz = lax.rem(chip + k, pairs)
                src = 2 * zz + core

                @pl.when(src < self.count)
                def _():
                    self.copy(src, pairs + zz, sibling).wait_send()

    class Reduce:
        def __init__(self, count, rows, psend, precv, fsend, frecv, sems, result):
            self.count, self.rows, self.part = count, rows, pl.ds(0, rows)
            self.psend, self.precv, self.fsend, self.frecv = psend, precv, fsend, frecv
            self.sems, self.result = sems, result

        def pair_copy(self, zz):
            return remote(
                self.psend.at[zz, self.part],
                self.precv.at[zz, self.part],
                self.sems.at[0, zz],
                self.sems.at[1, zz],
                expert=sibling,
            )

        def far_copy(self, zz, slot):
            return remote(
                self.fsend.at[zz, self.part],
                self.frecv.at[slot, self.part],
                self.sems.at[2, zz],
                self.sems.at[3, slot],
                expert=2 * zz + core,
            )

        def start(self, make):
            for k in range(pairs):
                zz = lax.rem(chip + 1 + k, pairs)
                block = 2 * zz + 1 - core

                @pl.when(block < self.count)
                def _():
                    self.psend[zz, self.part] = make(block).astype(BF16)
                    self.pair_copy(zz).start()

            for k in range(1, pairs):
                zz = lax.rem(chip + k, pairs)
                block = 2 * zz + core

                @pl.when(block < self.count)
                def _():
                    mine = make(block)
                    self.pair_copy(zz).wait_recv()
                    self.fsend[zz, self.part] = (
                        mine + self.precv[zz, self.part].astype(F32)
                    ).astype(BF16)
                    self.far_copy(zz, chip).start()

            @pl.when(me < self.count)
            def _():
                mine = make(me)
                self.pair_copy(chip).wait_recv()
                self.result[self.part] = mine + self.precv[chip, self.part].astype(F32)

            @pl.when(me >= self.count)
            def _():
                self.result[self.part] = jnp.zeros((self.rows, self.result.shape[1]), F32)

        def finish(self):
            @pl.when(me < self.count)
            def _():
                for k in range(1, pairs):
                    zz = lax.rem(chip + k, pairs)
                    self.far_copy(zz, zz).wait_recv()
                    self.result[self.part] += self.frecv[zz, self.part].astype(F32)

            for k in range(pairs):
                zz = lax.rem(chip + 1 + k, pairs)

                @pl.when(2 * zz + 1 - core < self.count)
                def _():
                    self.pair_copy(zz).wait_send()

            for k in range(1, pairs):
                zz = lax.rem(chip + k, pairs)

                @pl.when(2 * zz + core < self.count)
                def _():
                    self.far_copy(zz, chip).wait_send()

    def attn_weight_copy(peer, slot):
        ref = w_all.at[me, shard_rows(slot)]
        return remote(ref, ref, w_send.at[peer], w_recv.at[slot], dp=peer)

    def up_first(peer, slot):
        ref = up_w.at[shard_rows(high * n_low + slot)]
        return remote(ref, ref, uw_send.at[peer], uw_recv.at[slot], dp=high * n_low + peer)

    def up_second(peer, slot):
        ref = up_w.at[shard_rows(slot * n_low, n_low)]
        return remote(ref, ref, uw_send_two.at[peer], uw_recv_two.at[slot], dp=peer * n_low + low)

    def down_first(peer, slot):
        ref = down_w.at[shard_rows(slot * n_low + low)]
        return remote(ref, ref, dw_send.at[peer], dw_recv.at[slot], dp=peer * n_low + low)

    def down_second(peer, slot, block):
        ref = down_w.at[shard_rows(block * n_low + slot)]
        return remote(
            ref,
            ref,
            dw_send_two.at[peer, block],
            dw_recv_two.at[slot, block],
            dp=high * n_low + peer,
        )

    up_in = pltpu.make_async_copy(uw_hbm, ugrad_ref, in_sems.at[0])
    down_in = pltpu.make_async_copy(dw_hbm, dgrad_ref, in_sems.at[1])
    up_in.start()
    down_in.start()
    kv_k[...] = jnp.zeros_like(kv_k)
    barrier = pltpu.get_barrier_semaphore()
    for k in range(1, n_exp):
        pl.semaphore_signal(
            barrier, inc=1, device_id={"expert": lax.rem(me + k, n_exp)}, device_id_type=MESH
        )
    for k in range(1, n_dp):
        pl.semaphore_signal(
            barrier, inc=1, device_id={"dp": lax.rem(dp + k, n_dp)}, device_id_type=MESH
        )
    w_all[me, shard_rows(dp)] = aw_ref[...].astype(BF16)
    up_in.wait()
    up_w[shard_rows(dp)] = ugrad_ref[...].astype(BF16)
    down_in.wait()
    down_w[shard_rows(dp)] = dgrad_ref[...].astype(BF16)
    pl.semaphore_wait(barrier, n_exp + n_dp - 2)
    each_peer(lambda peer: attn_weight_copy(peer, dp).start())
    for peer in low_peers():
        up_first(peer, low).start()
    for peer in high_peers():
        down_first(peer, high).start()

    kvb[...] = kvw_ref[...].astype(BF16)
    rb[...] = rw_ref[...].astype(BF16)
    gain_one = vec_ref[0:1, :]
    bias_one = vec_ref[1:2, :]
    gain_two = vec_ref[2:3, :]
    bias_two = vec_ref[3:4, :]
    halt = vec_ref[4:5, :]
    state[0] = x_ref[...].astype(F32)
    own_rows = pl.ds(pl.multiple_of(me * own, own), own)

    lane = lax.broadcasted_iota(jnp.int32, (own, LANES), 1)
    route_lane = lax.broadcasted_iota(jnp.int32, (own, 2 * n_exp), 1)
    lane_two = lax.broadcasted_iota(jnp.int32, (2 * own, LANES), 1)
    lane_cap = lax.broadcasted_iota(jnp.int32, (cap, LANES), 1)
    route_cap = lax.broadcasted_iota(jnp.int32, (cap, 2 * n_exp), 1)

    def column(values, index, lanes):
        return jnp.sum(jnp.where(lanes == index, values, 0.0), axis=1, keepdims=True)

    def cap_rows(loop):
        return pl.ds(pl.multiple_of(loop * cap, cap), cap)

    def window_keys(loop):
        return kv_k[loop, pl.ds(win_at, window)].reshape(keys, 2 * HD)

    def routing():
        position = lax.broadcasted_iota(jnp.int32, (1, slots), 1)
        bound = 0
        segment = jnp.zeros((1, slots), F32)
        for index in range(len_ref.shape[1]):
            bound = bound + len_ref[0, index]
            segment = segment + jnp.where(position >= bound, 1.0, 0.0)
        sub = lax.broadcasted_iota(jnp.int32, (n_exp, slots), 0)
        position_all = lax.broadcasted_iota(jnp.int32, (n_exp, slots), 1)
        valid = segment < len_ref.shape[1] - 0.5
        rowm_ref[LOOPS] = segment
        picks, selected = [], jnp.zeros((n_exp, slots), F32)
        for loop in range(LOOPS):
            running = jnp.where(valid & (run_ref[...] > loop), 1.0, 0.0)
            att = jnp.zeros((n_exp, slots), F32)
            for k in range(ar_ref.shape[1]):
                att = att + jnp.where(ar_ref[loop, k : k + 1, :] == sub, 1.0, 0.0)
            ffn = jnp.zeros((n_exp, slots), F32)
            mine = jnp.zeros((1, slots), F32)
            for k in range(fr_ref.shape[1]):
                ffn = ffn + jnp.where(fr_ref[loop, k : k + 1, :] == sub, 1.0, 0.0)
                mine = mine + jnp.where(fr_ref[loop, k : k + 1, :] == me, running, 0.0)
            picks.append((att, ffn, running))
            selected = selected + jnp.where(sub == loop, mine, 0.0)
        ranks = selected
        shift = 1
        while shift < slots:
            moved = pltpu.roll(ranks, shift, 1)
            ranks = ranks + jnp.where(position_all >= shift, moved, 0.0)
            shift *= 2
        ranks = jnp.where(selected > 0.5, ranks - 1.0, -1.0)
        for loop in range(LOOPS):
            att, ffn, running = picks[loop]
            rank = ranks[loop : loop + 1]
            rowm_ref[loop] = rank
            rest = jnp.where(
                sub == 0,
                rank,
                jnp.where(sub == 1, running, jnp.where(sub == 2, segment, 0.0)),
            )
            spare = jnp.zeros((INFO - 3 * n_exp, slots), F32)
            meta_ref[loop] = jnp.transpose(jnp.concatenate([att, ffn, rest, spare], axis=0))

    def kv_copy(loop, where, sem):
        ref = kv_k.at[loop, me]
        return remote(ref, ref, kg_send.at[sem], kg_recv.at[me], expert=where)

    def prepare(loop):
        unit, _ = normalise(state[loop])
        normed = (unit * gain_one + bias_one).astype(BF16)
        normed_k[loop] = normed
        kv_k[loop, me] = nn(normed, kvb[...]).astype(BF16)
        for k in range(1, window):

            @pl.when(me + k < n_act)
            def _():
                kv_copy(loop, me + k, k - 1).start()

        info = meta_ref[loop, own_rows, 0 : 2 * n_exp]
        gate_k[loop] = masked_softmax(
            nt(normed, rb[...]), (info > 0.5) & (route_lane < n_exp)
        )

    def running_rows(loop):
        return meta_ref[loop, own_rows, RUN_LANE : RUN_LANE + 1]

    each_peer(lambda peer: attn_weight_copy(peer, peer).wait_recv())
    weights_gather = Gather(w_all, wg_send, wg_recv, n_exp)
    weights_gather.start()
    routing()
    prepare(0)
    seg_own = meta_ref[0, own_rows, SEG_LANE : SEG_LANE + 1]
    key_cols = pl.ds(pl.multiple_of(win_at * own, own), keys)
    seg_keys = rowm_ref[LOOPS, :, key_cols]
    row_at = me * own + lax.broadcasted_iota(jnp.int32, (own, keys), 0)
    key_at = win_at * own + lax.broadcasted_iota(jnp.int32, (own, keys), 1)
    allowed = (seg_own == seg_keys) & (key_at <= row_at)
    bias[...] = jnp.where(allowed, 0.0, masked_score)
    for peer in low_peers():
        up_first(peer, peer).wait_recv()
    for peer in high_peers():
        up_second(peer, high).start()
    for peer in high_peers():
        down_first(peer, peer).wait_recv()
    for peer in low_peers():
        for block in range(n_high):
            down_second(peer, low, block).start()
    down_acc[...] = jnp.zeros_like(down_acc)
    attn_acc[...] = jnp.zeros_like(attn_acc)
    small_acc[...] = jnp.zeros_like(small_acc)
    weights_gather.finish()

    def attention(loop):
        normed = normed_k[loop]

        def queries(expert, none):
            query = jnp.where(lane < HD, nn(normed, w_all[expert]), 0.0).astype(BF16)
            q_k[loop, pl.ds(pl.multiple_of(expert * own, own), own)] = query
            return none

        lax.fori_loop(0, n_exp, queries, 0)
        running = running_rows(loop)
        gates = gate_k[loop] * running
        mix[...] = jnp.zeros_like(mix)
        for k in range(1, window):

            @pl.when(active & (me >= k))
            def _():
                ref = kv_k.at[loop, me - k]
                remote(
                    ref, ref, kg_send.at[k - 1], kg_recv.at[me - k], expert=me - k
                ).wait_recv()

        kv_rows = window_keys(loop)

        def attend(pair, none):
            rows = pl.ds(pl.multiple_of(pair * 2 * own, 2 * own), 2 * own)
            scores = nt(q_k[loop, rows], kv_rows) * scale
            scores = (scores.reshape(2, own, keys) + bias[...][None]).reshape(2 * own, keys)
            powers = jnp.exp(scores - jnp.max(scores, axis=1, keepdims=True))
            prob = (powers * (1.0 / jnp.sum(powers, axis=1, keepdims=True))).astype(BF16)
            p_k[loop, rows] = prob
            outs = jnp.where(lane_two < HD, 0.0, nn(prob, kv_rows)).astype(BF16)
            o_k[loop, rows] = outs
            for half in range(2):
                expert = 2 * pair + half
                gate = column(gates, expert, route_lane)
                mix[...] += gate * nt(outs[half * own : (half + 1) * own], w_all[expert])
            return none

        lax.fori_loop(0, n_exp // 2, attend, 0)
        for k in range(1, window):

            @pl.when(me + k < n_act)
            def _():
                kv_copy(loop, me + k, k - 1).wait_send()

        centre = state[loop] + mix[...]
        middle[loop] = centre
        unit, _ = normalise(centre)
        second = (unit * gain_two + bias_two).astype(BF16)
        second_k[loop] = second
        rows_all[me] = second

    rows_gather = Gather(rows_all, ag_send, ag_recv, n_act)

    def place_matrices(loop):
        ranks = rowm_ref[loop, :, 0:valid_rows]
        slot = lax.broadcasted_iota(jnp.int32, (cap, valid_rows), 0).astype(F32)
        gather_m[...] = jnp.where(slot == ranks, 1.0, 0.0).astype(BF16)
        slot = lax.broadcasted_iota(jnp.int32, (own, cap), 1).astype(F32)

        def block_matrix(block, none):
            rows = pl.ds(pl.multiple_of(block * own, own), own)
            ranks = meta_ref[loop, rows, RANK_LANE : RANK_LANE + 1]
            scatter_m[rows] = jnp.where(slot == ranks, 1.0, 0.0).astype(BF16)
            return none

        lax.fori_loop(0, n_act, block_matrix, 0)

    def scatter_rows(block):
        return scatter_m[pl.ds(pl.multiple_of(block * own, own), own)]

    def take(buf):
        return nn(gather_m[...], buf[0:n_act].reshape(valid_rows, width))

    def expert_rows(loop, chosen):
        rows_in = take(rows_all).astype(BF16)
        rows_k[cap_rows(loop)] = rows_in
        allowed_lanes = (chosen > 0.5) & (route_cap >= n_exp)
        gate = column(masked_softmax(nt(rows_in, rb[...]), allowed_lanes), n_exp + me, route_cap)
        fgate_k[cap_rows(loop)] = gate
        part_k[cap_rows(loop)] = jnp.zeros((cap, width), F32)

    def chosen_rows(loop):
        return nn(gather_m[...], meta_ref[loop, 0:valid_rows, 0 : 2 * n_exp].astype(BF16))

    root = math.sqrt(2.0 / math.pi)

    def tile_cols(tile):
        return pl.ds(pl.multiple_of(tile * TILE, TILE), TILE)

    def hidden_layer(loop, with_slope):
        rows_in = rows_k[cap_rows(loop)]

        def step(tile, none):
            cols = tile_cols(tile)
            inner = nn(rows_in, up_w[:, cols])
            square = inner * inner
            curve = jnp.tanh(root * inner * (1.0 + 0.044715 * square))
            upper = 0.5 * (1.0 + curve)
            hidden = (inner * upper).astype(BF16)
            hid[cap_rows(loop), cols] = hidden
            if with_slope:
                gprime[cap_rows(loop), cols] = slope_of(inner, square, curve).astype(BF16)
            else:
                up_acc[0:cap, cols] = inner
            part_k[cap_rows(loop)] += nt(hidden, down_w[:, cols])
            return none

        lax.fori_loop(0, tiles, step, 0)

    def slope_of(inner, square, curve):
        return 0.5 * (1.0 + curve) + 0.5 * inner * (1.0 - curve * curve) * (
            root + (3.0 * 0.044715 * root) * square
        )

    def slopes(loop):
        def step(tile, none):
            cols = tile_cols(tile)
            inner = up_acc[0:cap, cols]
            square = inner * inner
            curve = jnp.tanh(root * inner * (1.0 + 0.044715 * square))
            gprime[cap_rows(loop), cols] = slope_of(inner, square, curve).astype(BF16)
            return none

        lax.fori_loop(0, tiles, step, 0)

    sums = Reduce(
        n_act, own, pair_send, pair_recv, far_send, far_recv, rs_sems, total
    )
    sums_two = Reduce(
        n_act,
        own,
        pair_send_two,
        pair_recv_two,
        far_send_two,
        far_recv_two,
        rs_sems_two,
        total_two,
    )
    back_sums = Reduce(
        n_act, own + EXTRA, pair_send, pair_recv, far_send, far_recv, rs_sems, total
    )

    def start_terms(loop, where):
        terms = (part_k[cap_rows(loop)] * fgate_k[cap_rows(loop)]).astype(BF16)
        where.start(lambda block: nn(scatter_rows(block), terms))

    def wait_weights():
        for peer in high_peers():
            up_second(peer, peer).wait_recv()
        for peer in low_peers():
            for block in range(n_high):
                down_second(peer, peer, block).wait_recv()

    def forward(loop, none):
        attention(loop)
        rows_gather.start()
        place_matrices(loop)
        chosen = chosen_rows(loop)

        @pl.when(loop == 0)
        def _():
            wait_weights()

        rows_gather.finish()
        expert_rows(loop, chosen)
        hidden_layer(loop, False)
        start_terms(loop, sums)
        slopes(loop)
        sums.finish()
        running = running_rows(loop)
        state[loop + 1] = jnp.where(running > 0.5, middle[loop] + total[0:own], state[loop])
        prepare(loop + 1)
        return none

    lax.fori_loop(0, last, forward, 0)

    cot = cot_ref[...].astype(F32)

    def chances():
        chance_one = jax.nn.sigmoid(jnp.sum(state[1] * halt, axis=1, keepdims=True))
        chance_two = jax.nn.sigmoid(jnp.sum(state[2] * halt, axis=1, keepdims=True))
        return chance_one, chance_two

    chance_one, chance_two = chances()
    sgrad[last] = ((1.0 - chance_one) * (1.0 - chance_two)) * cot
    rows_two[me] = (sgrad[last] * running_rows(last)).astype(BF16)
    back_gather = Gather(rows_two, bg_send, bg_recv, n_act)
    back_gather.start()
    carry[...] = jnp.zeros_like(carry)

    def finish_output():
        chance_one, chance_two = chances()
        first, next_one = state[1], state[2]
        final = jnp.where(running_rows(last) > 0.5, middle[last] + total_two[0:own], next_one)
        stay = 1.0 - chance_one
        weight_two = stay * chance_two
        weight_three = stay * (1.0 - chance_two)
        out_ref[...] = chance_one * first + weight_two * next_one + weight_three * final
        dot_one = jnp.sum(cot * first, axis=1, keepdims=True)
        dot_two = jnp.sum(cot * next_one, axis=1, keepdims=True)
        dot_three = jnp.sum(cot * final, axis=1, keepdims=True)
        slope_one = (chance_one * stay) * (
            dot_one - chance_two * dot_two - (1.0 - chance_two) * dot_three
        )
        slope_two = (chance_two * (1.0 - chance_two)) * stay * (dot_two - dot_three)
        sgrad[0] = chance_one * cot + slope_one * halt
        sgrad[1] = weight_two * cot + slope_two * halt
        small_acc[vec_at + 4 : vec_at + 5] = jnp.sum(
            slope_one * first + slope_two * next_one, axis=0, keepdims=True
        )

    vec_at = 2 * HD + EXTRA

    def expert_back(loop, grad_rows):
        gate = fgate_k[cap_rows(loop)]
        ggrad[...] = jnp.sum(grad_rows * part_k[cap_rows(loop)], axis=1, keepdims=True)
        scaled = (grad_rows * gate).astype(BF16)
        scaled_k[...] = scaled
        row_grads[...] = jnp.zeros_like(row_grads)

        def step(tile, none):
            cols = tile_cols(tile)
            inner_grad = (
                nn(scaled, down_w[:, cols]) * gprime[cap_rows(loop), cols].astype(F32)
            ).astype(BF16)
            gprime[cap_rows(loop), cols] = inner_grad
            row_grads[...] += nt(inner_grad, up_w[:, cols])
            return none

        lax.fori_loop(0, tiles, step, 0)
        terms = row_grads[...].astype(BF16)
        gate_grad = ggrad[...]
        upper = gate_grad.astype(BF16).astype(F32)
        spread = jnp.where(lane_cap == n_exp + me, upper, 0.0) + jnp.where(
            lane_cap == me, gate_grad - upper, 0.0
        )
        spread_t = jnp.transpose(spread)[0:EXTRA].astype(BF16)

        def row_terms(block):
            matrix = scatter_rows(block)
            grads = nt(spread_t, matrix)
            return jnp.concatenate(
                [
                    nn(matrix, terms),
                    jnp.concatenate([grads, jnp.zeros((EXTRA, width - own), F32)], axis=1),
                ],
                axis=0,
            )

        back_sums.start(row_terms)

    def expert_weights(loop):
        rows_in = rows_k[cap_rows(loop)]
        scaled = scaled_k[...]

        def step(tile, none):
            cols = tile_cols(tile)
            down_acc[:, cols] += tn(scaled, hid[cap_rows(loop), cols])
            up_acc[:, cols] += tn(rows_in, gprime[cap_rows(loop), cols])
            return none

        lax.fori_loop(0, tiles, step, 0)

    def order_at(source, receiver, count):
        return lax.rem(source - receiver + count, count) - 1

    spare = width // shard

    def up_grad_first(peer, slot, block, receiver):
        return remote(
            hid.at[shard_rows(block * n_low + peer)],
            u_first.at[order_at(slot, receiver, n_low), shard_rows(block)],
            ug_send.at[peer, block],
            ug_recv.at[slot, block],
            dp=high * n_low + peer,
        )

    def up_grad_second(peer, slot, receiver):
        return remote(
            hid.at[shard_rows(spare + peer)],
            u_last.at[order_at(slot, receiver, n_high)],
            ug_send_two.at[peer],
            ug_recv_two.at[slot],
            dp=peer * n_low + low,
        )

    def down_grad_first(peer, slot, receiver):
        return remote(
            gprime.at[shard_rows(peer * n_low, n_low)],
            d_first.at[order_at(slot, receiver, n_high)],
            dg_send.at[peer],
            dg_recv.at[slot],
            dp=peer * n_low + low,
        )

    def down_grad_second(peer, slot, receiver):
        return remote(
            gprime.at[shard_rows(spare + peer)],
            d_last.at[order_at(slot, receiver, n_low)],
            dg_send_two.at[peer],
            dg_recv_two.at[slot],
            dp=high * n_low + peer,
        )

    def send_expert_weights():
        hid[0:width] = up_acc[...].astype(BF16)
        for peer in low_peers():
            for block in range(n_high):
                up_grad_first(peer, low, block, peer).start()
        gprime[0:width] = down_acc[...].astype(BF16)
        for peer in high_peers():
            down_grad_first(peer, high, peer).start()

    def pass_expert_weights():
        for peer in low_peers():
            for block in range(n_high):
                up_grad_first(peer, peer, block, low).wait_recv()
        for block in range(n_high):
            added = up_acc[shard_rows(block * n_low + low)]
            for peer in low_peers():
                added = added + u_first[
                    order_at(peer, low, n_low), shard_rows(block)
                ].astype(F32)
            hid[shard_rows(spare + block)] = added.astype(BF16)
        for peer in high_peers():
            up_grad_second(peer, high, peer).start()
        for peer in high_peers():
            down_grad_first(peer, peer, high).wait_recv()
        for block in range(n_low):
            added = down_acc[shard_rows(high * n_low + block)]
            for peer in high_peers():
                added = added + d_first[
                    order_at(peer, high, n_high), shard_rows(block)
                ].astype(F32)
            gprime[shard_rows(spare + block)] = added.astype(BF16)
        for peer in low_peers():
            down_grad_second(peer, low, peer).start()

    def finish_expert_weights():
        added = hid[shard_rows(spare + high)].astype(F32)
        for peer in high_peers():
            up_grad_second(peer, peer, high).wait_recv()
            added = added + u_last[order_at(peer, high, n_high)].astype(F32)
        ugrad_ref[...] = added
        added = gprime[shard_rows(spare + low)].astype(F32)
        for peer in low_peers():
            down_grad_second(peer, peer, low).wait_recv()
            added = added + d_last[order_at(peer, low, n_low)].astype(F32)
        dgrad_ref[...] = added

    attn_sums = Reduce(
        n_exp,
        2 * HD,
        pair_send_two,
        pair_recv_two,
        far_send_two,
        far_recv_two,
        a_sems,
        total_two,
    )

    def dkv_copy(distance, owner):
        return remote(
            dkv_send.at[jnp.clip(owner - win_at, 0, window - 1)],
            dkv_recv.at[distance - 1],
            dk_send.at[distance - 1],
            dk_recv.at[distance - 1],
            expert=owner,
        )

    def attention_back(loop):
        info = meta_ref[loop, own_rows, 0 : 2 * n_exp]
        running = running_rows(loop)
        branch = (sgrad[loop] + carry[...]) * running
        second_grad = total[0:own]
        gate_rows = total[own : own + n_exp, 0:own] + total[own + n_exp : own + 2 * n_exp, 0:own]
        gate_rows = jnp.concatenate(
            [jnp.zeros((n_exp, own), F32), gate_rows, jnp.zeros((LANES - 2 * n_exp, own), F32)],
            axis=0,
        )
        gate_grads = jnp.transpose(gate_rows)[:, 0 : 2 * n_exp]
        second = second_k[loop]
        gates = masked_softmax(nt(second, rb[...]), (info > 0.5) & (route_lane >= n_exp))
        logit_grad = (
            gates * (gate_grads - jnp.sum(gates * gate_grads, axis=1, keepdims=True))
        ).astype(BF16)
        second_grad = second_grad + nn(logit_grad, rb[...])
        unit, inverse = normalise(middle[loop])
        middle_grad = norm_back(second_grad, unit, inverse, gain_two) + branch
        mgrad[...] = middle_grad

        gates = gate_k[loop]
        kv_rows = window_keys(loop)
        dkv_t[...] = jnp.zeros_like(dkv_t)

        def scores_back(pair, none):
            rows = pl.ds(pl.multiple_of(pair * 2 * own, 2 * own), 2 * own)
            out_grads = []
            for half in range(2):
                expert = 2 * pair + half
                part_grad = (column(gates, expert, route_lane) * mgrad[...]).astype(BF16)
                out_grads.append(
                    jnp.where(lane < HD, 0.0, nn(part_grad, w_all[expert])).astype(BF16)
                )
            out_grad = jnp.concatenate(out_grads, axis=0)
            prob_low = p_k[loop, rows]
            prob = prob_low.astype(F32)
            prob_grad = nt(out_grad, kv_rows)
            centre = jnp.sum(prob * prob_grad, axis=1, keepdims=True)
            score_grad = (prob * (prob_grad - centre)).astype(BF16)
            ds_k[rows] = score_grad
            dkv_t[...] += tn(q_k[loop, rows], score_grad) * scale + tn(out_grad, prob_low)
            return none

        lax.fori_loop(0, n_exp // 2, scores_back, 0)
        for block in range(window):
            grads = jnp.transpose(dkv_t[:, block * own : (block + 1) * own])
            dkv[block] = grads
            dkv_send[block] = grads.astype(BF16)
        for distance in range(1, window):

            @pl.when(active & (me >= distance))
            def _():
                dkv_copy(distance, me - distance).start()

        small_acc[2 * HD : vec_at] += tn(logit_grad, second)
        small_acc[vec_at + 2 : vec_at + 3] += jnp.sum(second_grad * unit, axis=0, keepdims=True)
        small_acc[vec_at + 3 : vec_at + 4] += jnp.sum(second_grad, axis=0, keepdims=True)
        normed = normed_k[loop]
        mix[...] = jnp.zeros_like(mix)
        dga[...] = jnp.zeros_like(dga)

        def queries_back(pair, none):
            rows = pl.ds(pl.multiple_of(pair * 2 * own, 2 * own), 2 * own)
            outs = o_k[loop, rows]
            query_grad = jnp.where(lane_two < HD, nn(ds_k[rows], kv_rows) * scale, 0.0).astype(BF16)
            for half in range(2):
                expert = 2 * pair + half
                cut = slice(half * own, (half + 1) * own)
                middle_grad = mgrad[...]
                dot = jnp.sum(middle_grad * nt(outs[cut], w_all[expert]), axis=1, keepdims=True)
                dga[...] += jnp.where(route_lane == expert, dot, 0.0)
                part_grad = (column(gates, expert, route_lane) * middle_grad).astype(BF16)
                attn_acc[expert] += tn(query_grad[cut], normed) + tn(outs[cut], part_grad)
                mix[...] += nt(query_grad[cut], w_all[expert])
            return none

        lax.fori_loop(0, n_exp // 2, queries_back, 0)

        @pl.when(loop == 0)
        def _():
            attn_sums.start(lambda block: attn_acc[block])

        gate_grads = dga[...]
        logit_grad = (
            gates * (gate_grads - jnp.sum(gates * gate_grads, axis=1, keepdims=True))
        ).astype(BF16)
        small_acc[2 * HD : vec_at] += tn(logit_grad, normed)
        normed_grad = mix[...] + nn(logit_grad, rb[...])
        unit, inverse = normalise(state[loop])

        own_block = jnp.clip(me - win_at, 0, window - 1)
        dkv[window] = jnp.where(active, dkv[own_block], 0.0)
        for distance in range(1, window):

            @pl.when(me + distance < n_act)
            def _():
                remote(
                    dkv_send.at[0],
                    dkv_recv.at[distance - 1],
                    dk_send.at[distance - 1],
                    dk_recv.at[distance - 1],
                    expert=me + distance,
                ).wait_recv()
                dkv[window] += dkv_recv[distance - 1].astype(F32)

        for distance in range(1, window):

            @pl.when(active & (me >= distance))
            def _():
                dkv_copy(distance, me - distance).wait_send()

        kv_grad = dkv[window].astype(BF16)
        small_acc[0 : 2 * HD] += tn(kv_grad, normed)
        normed_grad = normed_grad + nt(kv_grad, kvb[...])
        small_acc[vec_at : vec_at + 1] += jnp.sum(normed_grad * unit, axis=0, keepdims=True)
        small_acc[vec_at + 1 : vec_at + 2] += jnp.sum(normed_grad, axis=0, keepdims=True)
        carry[...] = (
            (sgrad[loop] + carry[...]) * (1.0 - running)
            + mgrad[...]
            + norm_back(normed_grad, unit, inverse, gain_one)
        )

    attention(last)
    rows_gather.start()
    up_acc[...] = jnp.zeros_like(up_acc)
    place_matrices(last)
    chosen = chosen_rows(last)
    back_gather.finish()
    grad_rows = take(rows_two)
    rows_gather.finish()
    expert_rows(last, chosen)
    hidden_layer(last, True)
    expert_back(last, grad_rows)
    start_terms(last, sums_two)
    expert_weights(last)
    back_sums.finish()
    attention_back(last)
    sums_two.finish()
    finish_output()

    def backward(step, none):
        loop = last - 1 - step
        branch = (sgrad[loop] + carry[...]) * running_rows(loop)
        rows_all[me] = branch.astype(BF16)
        rows_gather.start()
        place_matrices(loop)
        rows_gather.finish()
        expert_back(loop, take(rows_all))
        expert_weights(loop)

        @pl.when(loop == 0)
        def _():
            send_expert_weights()

        back_sums.finish()
        attention_back(loop)
        return none

    lax.fori_loop(0, last, backward, 0)
    xgrad_ref[...] = carry[...]

    chunk = small_acc.shape[0] // n_exp
    small_sums = Reduce(
        n_exp, chunk, s_pair_send, s_pair_recv, s_far_send, s_far_recv, s_sems, s_total
    )
    small_sums.start(lambda block: small_acc[pl.ds(pl.multiple_of(block * chunk, chunk), chunk)])
    pass_expert_weights()
    attn_sums.finish()
    a_total[...] = jnp.transpose(total_two[...])
    a_stage[...] = a_total[...].astype(BF16)

    def attn_copy(peer, slot):
        return remote(
            a_stage.at[shard_rows(peer)],
            a_recv.at[shard_rows(slot)],
            t_send.at[1, peer],
            t_recv.at[1, slot],
            dp=peer,
        )

    def small_copy(peer, slot):
        return remote(
            s_dp.at[slot], s_dp.at[slot], t_send.at[0, peer], t_recv.at[0, slot], dp=peer
        )

    small_sums.finish()
    s_dp[dp] = s_total[...].astype(BF16)
    each_peer(lambda peer: small_copy(peer, dp).start())
    each_peer(lambda peer: attn_copy(peer, dp).start())
    each_peer(lambda peer: small_copy(peer, peer).wait_recv())
    s_total[...] = jnp.zeros_like(s_total)

    def add_small(index, none):
        s_total[...] += s_dp[index].astype(F32)
        return none

    lax.fori_loop(0, n_dp, add_small, 0)
    s_all[me] = s_total[...]
    small_gather = Gather(s_all, sg_send, sg_recv, n_exp)
    small_gather.start()
    agrad_ref[...] = a_total[shard_rows(dp)]

    def add_attn(peer):
        attn_copy(peer, peer).wait_recv()
        agrad_ref[...] += a_recv[shard_rows(peer)].astype(F32)

    each_peer(add_attn)
    finish_expert_weights()
    small_gather.finish()
    small = s_all[...].reshape(n_exp * chunk, width)
    kvgrad_ref[...] = jnp.transpose(small[0 : 2 * HD])
    rgrad_ref[...] = small[2 * HD : vec_at]
    vgrad_ref[...] = small[vec_at : vec_at + 8]

    def sent(peer):
        attn_weight_copy(peer, dp).wait_send()
        small_copy(peer, dp).wait_send()
        attn_copy(peer, dp).wait_send()

    each_peer(sent)
    for peer in low_peers():
        up_first(peer, low).wait_send()
        down_grad_second(peer, low, peer).wait_send()
        for block in range(n_high):
            down_second(peer, low, block).wait_send()
            up_grad_first(peer, low, block, peer).wait_send()
    for peer in high_peers():
        down_first(peer, high).wait_send()
        up_second(peer, high).wait_send()
        up_grad_second(peer, high, peer).wait_send()
        down_grad_first(peer, high, peer).wait_send()


def adam_kernel(*refs):
    out_in, xgrad_in, ugrad, dgrad, agrad, kvgrad, rgrad, vgrad = refs[:8]
    shared, kv, router, attn, up, down = (refs[8 + 3 * index : 11 + 3 * index] for index in range(6))
    out, xgrad = refs[26:28]
    shared_out, kv_out, router_out, attn_out, up_out, down_out = (
        refs[28:31],
        refs[31:34],
        refs[34:37],
        refs[37:41],
        refs[41:45],
        refs[45:49],
    )

    def update(sources, grad, results, rate, decay):
        values = adam_update(*(source[...] for source in sources), grad, rate, decay)
        for result, value in zip(results, values):
            result[...] = value
        if len(results) > 3:
            results[3][...] = values[0].astype(BF16)

    out[...] = out_in[...]
    xgrad[...] = xgrad_in[...]
    update(up, ugrad[...], up_out, 14.0 / math.sqrt(D), decay_rate)
    update(down, dgrad[...], down_out, 17.0 / math.sqrt(FF), decay_rate)

    @pl.when(pl.program_id(0) == 0)
    def _():
        row = lax.broadcasted_iota(jnp.int32, shared[0].shape, 0)
        rates = jnp.where(row < 4, 6.0, 20.0 / math.sqrt(D))
        update(shared, vgrad[0 : shared[0].shape[0]], shared_out, rates, 0.0)
        update(kv, kvgrad[...], kv_out, 20.0 / math.sqrt(D), decay_rate)
        update(router, rgrad[...], router_out, 50.0 / math.sqrt(3 * D), decay_rate)
        lane = lax.broadcasted_iota(jnp.int32, attn[0].shape, 1)
        rates = jnp.where(lane < HD, 25.0 / math.sqrt(D), 50.0 / math.sqrt(HD))
        update(attn, agrad[...], attn_out, rates, decay_rate)


def dp_grid(n_dp):
    n_low = 1
    while n_low * n_low * 4 <= n_dp:
        n_low *= 2
    return n_low, n_dp // n_low


def per_device(
    block_input,
    cotangent,
    lengths,
    run_loops,
    attn_routes,
    ffn_routes,
    shared_vectors,
    shared_moment,
    shared_second,
    key_value,
    kv_moment,
    kv_second,
    router_weights,
    router_moment,
    router_second,
    attn_weights,
    attn_moment,
    attn_second,
    up_weights,
    up_moment,
    up_second,
    down_weights,
    down_moment,
    down_second,
):
    n_exp = lax.axis_size("expert")
    n_dp = lax.axis_size("dp")
    own, width = block_input.shape
    slots = run_loops.shape[0]
    shard = attn_weights.shape[1]
    hidden = up_weights.shape[2]
    cap = 5 * slots * KFF // (4 * n_exp)
    n_act = FILLED // own
    window = min(n_act, MAXLEN // own + 1)
    pairs = n_exp // 2
    valid_rows = n_act * own
    n_low, n_high = dp_grid(n_dp)

    small_rows = 32 * n_exp
    vmem = pltpu.VMEM
    dma = pltpu.SemaphoreType.DMA
    block = (pairs, own + EXTRA, width)
    small_block = (pairs, 32, width)
    scratch = [
        vmem((LOOPS, slots, INFO), F32),
        vmem((LOOPS + 1, 1, slots), F32),
        vmem((width, 2 * HD), BF16),
        vmem((2 * n_exp, width), BF16),
        vmem((n_exp, width, 2 * HD), BF16),
        vmem((width, hidden), BF16),
        vmem((width, hidden), BF16),
        vmem((width, hidden), F32),
        vmem((width, hidden), F32),
        vmem((n_exp, 2 * HD, width), F32),
        vmem((small_rows, width), F32),
        vmem((LOOPS, own, width), F32),
        vmem((LOOPS, own, width), F32),
        vmem((LOOPS, own, width), BF16),
        vmem((LOOPS, own, width), BF16),
        vmem((LOOPS, n_exp, own, 2 * HD), BF16),
        vmem((LOOPS, n_exp * own, 2 * HD), BF16),
        vmem((LOOPS, n_exp * own, 2 * HD), BF16),
        vmem((LOOPS, n_exp * own, window * own), BF16),
        vmem((n_exp * own, window * own), BF16),
        vmem((own, window * own), F32),
        vmem((own, width), F32),
        vmem((own, 2 * n_exp), F32),
        vmem((2 * HD, window * own), F32),
        vmem((window + 1, own, 2 * HD), F32),
        vmem((LOOPS, own, 2 * n_exp), F32),
        vmem((n_exp, own, width), BF16),
        vmem((n_exp, own, width), BF16),
        vmem((cap, valid_rows), BF16),
        vmem((valid_rows, cap), BF16),
        vmem((LOOPS * cap, width), BF16),
        vmem((LOOPS * cap, hidden), BF16),
        vmem((LOOPS * cap, hidden), BF16),
        vmem((cap, width), F32),
        vmem((LOOPS * cap, width), F32),
        vmem((LOOPS * cap, 1), F32),
        vmem((cap, 1), F32),
        vmem((cap, width), BF16),
        vmem((LOOPS, own, width), F32),
        vmem((own, width), F32),
        vmem((own, width), F32),
        vmem((own + EXTRA, width), F32),
        vmem((own, width), F32),
        vmem(block, BF16),
        vmem(block, BF16),
        vmem(block, BF16),
        vmem(block, BF16),
        vmem((pairs, own, width), BF16),
        vmem((pairs, own, width), BF16),
        vmem((pairs, own, width), BF16),
        vmem((pairs, own, width), BF16),
        vmem((window, own, 2 * HD), BF16),
        vmem((window, own, 2 * HD), BF16),
        vmem((n_low - 1, n_high * shard, hidden), BF16),
        vmem((n_high - 1, shard, hidden), BF16),
        vmem((n_high - 1, n_low * shard, hidden), BF16),
        vmem((n_low - 1, shard, hidden), BF16),
        vmem((width, 2 * HD), F32),
        vmem((width, 2 * HD), BF16),
        vmem((width, 2 * HD), BF16),
        vmem(small_block, BF16),
        vmem(small_block, BF16),
        vmem(small_block, BF16),
        vmem(small_block, BF16),
        vmem((32, width), F32),
        vmem((n_dp, 32, width), BF16),
        vmem((n_exp, 32, width), F32),
        dma((2,)),
        dma((n_dp,)),
        dma((n_dp,)),
        dma((n_low,)),
        dma((n_low,)),
        dma((n_high,)),
        dma((n_high,)),
        dma((n_high,)),
        dma((n_high,)),
        dma((n_low, n_high)),
        dma((n_low, n_high)),
        dma((2 * pairs,)),
        dma((n_exp,)),
        dma((2 * pairs,)),
        dma((n_exp,)),
        dma((2 * pairs,)),
        dma((n_exp,)),
        dma((2 * pairs,)),
        dma((n_exp,)),
        dma((window,)),
        dma((n_exp,)),
        dma((4, pairs)),
        dma((4, pairs)),
        dma((4, pairs)),
        dma((4, pairs)),
        dma((window,)),
        dma((window,)),
        dma((n_low, n_high)),
        dma((n_low, n_high)),
        dma((n_high,)),
        dma((n_high,)),
        dma((n_high,)),
        dma((n_high,)),
        dma((n_low,)),
        dma((n_low,)),
        dma((2, n_dp)),
        dma((2, n_dp)),
    ]
    whole = pl.BlockSpec(memory_space=pltpu.VMEM)
    scalars = pl.BlockSpec(memory_space=pltpu.SMEM)
    outside = pl.BlockSpec(memory_space=pl.ANY)
    shape = jax.ShapeDtypeStruct
    sums = pl.pallas_call(
        functools.partial(block_kernel, n_exp, n_dp, n_act, cap),
        out_shape=(
            shape((own, width), F32),
            shape((own, width), F32),
            shape((shard, hidden), F32),
            shape((shard, hidden), F32),
            shape((shard, 2 * HD), F32),
            shape((width, 2 * HD), F32),
            shape((2 * n_exp, width), F32),
            shape((8, width), F32),
        ),
        in_specs=[whole, whole, scalars, *([whole] * 7), outside, outside],
        out_specs=[whole] * 8,
        scratch_shapes=scratch,
        compiler_params=pltpu.CompilerParams(
            collective_id=0, has_side_effects=True, vmem_limit_bytes=63 * 1024 * 1024
        ),
        name="block",
    )(
        block_input,
        cotangent,
        lengths,
        run_loops[None],
        attn_routes.transpose(0, 2, 1),
        ffn_routes.transpose(0, 2, 1),
        shared_vectors,
        key_value,
        router_weights.T,
        attn_weights[0],
        up_weights[0],
        down_weights[0],
    )

    steps = max(1, shard // 16)
    rows = shard // steps

    def by_rows(array):
        return pl.BlockSpec((array.shape[0] // steps, array.shape[1]), lambda step: (step, 0))

    def fixed(array):
        return pl.BlockSpec(array.shape, lambda step: (0, 0))

    output, input_grad, up_sum, down_sum, *small = sums
    small_args = [
        shared_vectors,
        shared_moment,
        shared_second,
        key_value,
        kv_moment,
        kv_second,
        router_weights.T,
        router_moment.T,
        router_second.T,
        attn_weights[0],
        attn_moment[0],
        attn_second[0],
    ]
    large_args = [
        up_weights[0],
        up_moment[0],
        up_second[0],
        down_weights[0],
        down_moment[0],
        down_second[0],
    ]
    attn_low = shape((shard, 2 * HD), BF16)
    large_low = shape((shard, hidden), BF16)
    like = [shape(array.shape, array.dtype) for array in small_args]
    big = [shape(array.shape, array.dtype) for array in large_args]
    outs = [
        shape(output.shape, F32),
        shape(input_grad.shape, F32),
        *like,
        attn_low,
        *big[:3],
        large_low,
        *big[3:],
        large_low,
    ]
    results = pl.pallas_call(
        adam_kernel,
        grid=(steps,),
        out_shape=outs,
        in_specs=[
            by_rows(output),
            by_rows(input_grad),
            by_rows(up_sum),
            by_rows(down_sum),
            *(fixed(array) for array in small),
            *(fixed(array) for array in small_args),
            *(by_rows(array) for array in large_args),
        ],
        out_specs=[
            by_rows(output),
            by_rows(input_grad),
            *(fixed(array) for array in (*like, attn_low)),
            *(by_rows(array) for array in (*big[:3], large_low, *big[3:], large_low)),
        ],
        name="adamw",
    )(*sums, *small_args, *large_args)
    output, input_grad, *rest = results
    shared_kv, router, weights = rest[:6], rest[6:9], rest[9:]
    return (
        output,
        input_grad,
        *shared_kv,
        *(array.T for array in router),
        *(array[None] for array in weights),
    )


def solution(mesh):
    rows = P(("dp", "expert"), None)
    weights = P("expert", "dp", None)
    return jax.shard_map(
        per_device,
        mesh=mesh,
        in_specs=(
            rows,
            rows,
            P("dp", None),
            P("dp"),
            P(None, "dp", None),
            P(None, "dp", None),
            *([P()] * 9),
            *([weights] * 9),
        ),
        out_specs=(rows, rows, *([P()] * 9), *([weights] * 12)),
        check_vma=False,
    )
```

time: 367 us -> 292 us (0.80)
  Pallas kernels: 337 us -> 291 us
  other arithmetic: 25.2 us -> 0 us
  local copies, waits for them, and re-layouts: 3.95 us -> 0 us
    pallas_call x1, Pallas kernels: 337 us -> 280 us  [per_device(): pl.pallas_call(functools.partial(block_kernel, n_exp, n_dp, n_act, cap),...]
    pallas_call x0 -> x1, Pallas kernels: none -> 10.9 us  [per_device(): pl.pallas_call(adam_kernel, grid=(steps,), out_shape=outs, in_specs=[by_r...]
    convert_element_type x7 -> x0, other arithmetic: 9.67 us -> none  [the longest x1 4.44 us: per_device(): up_new[0].astype(BF16)]
    reduce_or x3 -> x0, other arithmetic: 6.52 us -> none  [the longest x1 4.39 us: per_device(): jnp.any(attn_routes[..., None] == lane, axis=2)]
    sub x3 -> x0, other arithmetic: 3.8 us -> none  [adam_update(): weight - rate * (moment_hat / (jnp.sqrt(second_hat) + adam_eps) + decay *...]
where the time goes in v2:
time: 292 us
  Pallas kernels  291 us (100%)
    pallas_call x1, Pallas kernels, per_device(): pl.pallas_call(functools.partial(block_kernel, n_exp, n_dp, n_act, cap),...  280 us
    pallas_call x1, Pallas kernels, per_device(): pl.pallas_call(adam_kernel, grid=(steps,), out_shape=outs, in_specs=[by_r...  10.9 us

profile of v2, /device:TPU:0, one launch (start us, length us, event | category | flops | bytes accessed | tf_op | source)
XLA Modules:
  0.0 291.6 jit_solution(14844403793580835121)
XLA Ops:
  0.7 279.9 %block.1 = (f32[128,512]{1,0:T(8,128)}, f32[128,512]{1,0:T(8,128)}, f32[128,2048]{1,0:T(8,128)}, f32[128,2048]{1,0:T(8,128)}, f32[128,128]{1,0:T(8,128)}, /*inde...) custom-call(bf16[128,512]{1,0:T(8,128)(2,1)} %x_ref.1, bf16[128,512]{1,0:T(8,128)(2,1)} %cot_ref.1, ...), custom_call_target="tpu_custom_call" | custom-call | tf_op jit(solution)/shard_map/block/pallas_call | solution.py:1359
  280.6 10.9 %adamw.1 = (f32[128,512]{1,0:T(8,128)}, f32[128,512]{1,0:T(8,128)}, f32[5,512]{1,0:T(8,128)}, f32[5,512]{1,0:T(8,128)}, f32[5,512]{1,0:T(8,128)}, /*index=5*/f32...) custom-call(f32[128,512]{1,0:T(8,128)} %get-tuple-element.54.refs_0_, ...), custom_call_target="tpu_custom_call" | custom-call | tf_op jit(solution)/shard_map/adamw/pallas_call | solution.py:1439
